TPU v7x, 32 devices: a whole 2x2x4 slice. The times are simulated.
32 devices in a mesh: mp: 8 (over y, x, core), batch: 4 (over z).
Axes of the slice: x: 2, y: 2, z: 4, core: 2. Of those that a mesh axis runs over, the one named last changes fastest.
Arguments:
- inputs: bfloat16 [24, 12288], P('mp', 'batch'), may hold values from -6 to 6
- weight: bfloat16 [12288, 49152], P('batch', 'mp'), may hold values from -0.0546875 to 0.0546875
- out_grad: bfloat16 [24, 49152], P('batch', 'mp'), may hold values from -6 to 6
- pre_act: bfloat16 [24, 49152], P('batch', 'mp'), may hold values from -6 to 6
Outputs:
- input_grad: bfloat16 [24, 12288], P('mp', 'batch')
- weight_grad: bfloat16 [12288, 49152], P('batch', 'mp')
All inputs are finite; a program needn't handle non-finite values.
Results may differ from a plain program's by a relative error of at most 0.0049.
Values may be sent and summed in bfloat16 or wider, within the bound.
No kernel may reach another device: no remote copies, remote signals or barrier semaphores. Data moves between devices by JAX's collectives and lax.ppermute only.
A program may use at most 256 MiB of HBM per device.

v0:
```python
import jax
import jax.numpy as jnp
from jax import lax
from jax.sharding import PartitionSpec as P


def gelu_back(pre_act, out_grad):
    value, pullback = jax.vjp(
        lambda v: jax.nn.gelu(v, approximate=True), pre_act.astype(jnp.float32)
    )
    return pullback(out_grad.astype(jnp.float32))[0].astype(jnp.bfloat16)


def shards(inputs, weight, out_grad, pre_act):
    all_grad, all_pre = (
        lax.all_gather(out_grad, "batch", axis=0, tiled=True),
        lax.all_gather(pre_act, "batch", axis=0, tiled=True),
    )
    hidden_grad = gelu_back(all_pre, all_grad)
    rows = hidden_grad
    weight_grad = lax.dot_general(
        lax.all_gather(inputs, "mp", axis=0, tiled=True),
        rows,
        (((0,), (0,)), ((), ())),
        preferred_element_type=jnp.float32,
    ).astype(jnp.bfloat16)
    rows = hidden_grad
    input_grad = lax.psum_scatter(
        lax.dot_general(rows, weight, (((1,), (1,)), ((), ())), preferred_element_type=jnp.float32),
        "mp",
        scatter_dimension=0,
        tiled=True,
    ).astype(jnp.bfloat16)
    return (input_grad, weight_grad)


def solution(mesh):
    return jax.shard_map(
        shards,
        mesh=mesh,
        in_specs=(P("mp", "batch"), P("batch", "mp"), P("batch", "mp"), P("batch", "mp")),
        out_specs=(P("mp", "batch"), P("batch", "mp")),
        check_vma=False,
    )
```

profile of v0, /device:TPU:0, one launch (start us, length us, event | category | flops | bytes accessed | tf_op | source)
XLA Modules:
  0.0 151.6 jit_solution(8199231894790621963)
XLA Ops:
  0.6 1.2 dynamic-slice
  2.5 10.9 %all-gather.2 = bf16[8,3,3072]{2,1,0:T(4,128)(2,1)S(1)} all-gather(bf16[1,3,3072]{2,1,0:T(4,128)(2,1)} %bitcast.12), channel_id=1, replica_groups=mesh['mp'=8,'batch'=4] {'mp'}, dimensions={0}, use_global_device_ids=true | all-gather | bytes 165888 | tf_op jit(solution)/shard_map/all_gather | solution.py:22
  13.4 0.1 reshape.9
  13.6 15.1 %all-gather = bf16[4,6,6144]{2,1,0:T(8,128)(2,1)S(1)} all-gather(bf16[1,6,6144]{2,1,0:T(8,128)(2,1)} %bitcast.10), channel_id=1, replica_groups=mesh['mp'=8,'batch'=4] {'batch'}, dimensions={0}, use_global_device_ids=true | all-gather | bytes 368640 | tf_op jit(solution)/shard_map/all_gather | solution.py:16
  28.7 0.1 reshape.10
  28.8 15.6 %all-gather.1 = bf16[4,6,6144]{2,1,0:T(8,128)(2,1)S(1)} all-gather(bf16[1,6,6144]{2,1,0:T(8,128)(2,1)} %bitcast.11), channel_id=1, replica_groups=mesh['mp'=8,'batch'=4] {'batch'}, dimensions={0}, use_global_device_ids=true | all-gather | bytes 368640 | tf_op jit(solution)/shard_map/all_gather | solution.py:17
  44.4 0.1 reshape.11
  44.5 0.4 fusion.6
  44.9 15.9 %fusion.7 = f32[24,3072]{1,0:T(8,128)S(1)} fusion(bf16[24,6144]{1,0:T(8,128)(2,1)S(1)} %fusion.6, bf16[3072,6144]{1,0:T(8,128)(2,1)} %param.5), kind=kOutput, calls=%fused_computation.11 | convolution fusion | flops 905969664 | bytes 38338560 | tf_op jit(solution)/shard_map/dot_general | solution.py:29
  60.9 25.5 %all-reduce.2 = bf16[24,3072]{1,0:T(8,128)(2,1)S(1)} all-reduce(f32[24,3072]{1,0:T(8,128)S(1)} %fusion.7), channel_id=2, replica_groups=mesh['mp'=8,'batch'=4] {'mp'}, use_global_device_ids=true, to_apply=%region_0.0.clone | all-reduce | flops 73728 | bytes 442368
  86.3 0.6 dynamic-slice_convert_fusion
  87.0 16.1 %convert_bitcast_fusion = bf16[3072,6144]{0,1:T(8,128)(2,1)} fusion(bf16[24,6144]{1,0:T(8,128)(2,1)S(1)} %fusion.6, bf16[24,3072]{1,0:T(8,128)(2,1)S(1)} %reshape.9), kind=kOutput, calls=%fused_computation | convolution fusion | flops 924844032 | bytes 38191104 | tf_op jit(solution)/shard_map/dot_general | solution.py:21
  103.1 48.5 %copy.8 = bf16[3072,6144]{1,0:T(8,128)(2,1)} copy(bf16[3072,6144]{0,1:T(8,128)(2,1)} %convert_bitcast_fusion) | data formatting | bytes 75497472
where the time goes:
time: 153 us; the launch traced here: 152 us
  blocking collectives  67.1 us (44%)
  local copies, waits for them, and re-layouts  50.7 us (33%)
  matrix products  32 us (21%)
    unnamed x3, local copies, waits for them, and re-layouts  49.9 us
    unnamed x1, blocking collectives  25.5 us
    dot_general x1, matrix products, shards(): lax.dot_general(lax.all_gather(inputs, 'mp', axis=0, tiled=True), rows, (...  16.1 us
    dot_general x1, matrix products, shards(): lax.dot_general(rows, weight, (((1,), (1,)), ((), ())), preferred_element...  15.9 us
    all_gather x1, blocking collectives, shards(): lax.all_gather(pre_act, 'batch', axis=0, tiled=True)  15.6 us
    all_gather x1, blocking collectives, shards(): lax.all_gather(out_grad, 'batch', axis=0, tiled=True)  15.1 us
    all_gather x1, blocking collectives, shards(): lax.all_gather(inputs, 'mp', axis=0, tiled=True)  10.9 us

commit v1 on v0

v1 whole, which is shorter than its diff:
```python
import functools

import jax
import jax.numpy as jnp
from jax import lax
from jax.experimental import pallas as pl
from jax.experimental.pallas import tpu as pltpu
from jax.sharding import PartitionSpec as P

F32, BF16 = jnp.float32, jnp.bfloat16
MIB = 1 << 20
ROWS = 8
VMEM = pl.BlockSpec(memory_space=pltpu.VMEM)
SMEM = pl.BlockSpec(memory_space=pltpu.SMEM)
ANY = pl.BlockSpec(memory_space=pl.ANY)


def gelu_back(pre_act, out_grad):
    value, pullback = jax.vjp(
        lambda v: jax.nn.gelu(v, approximate=True), pre_act.astype(F32)
    )
    return pullback(out_grad.astype(F32))[0].astype(BF16)


def exchange(x, axis, size, bits):
    return lax.ppermute(x, axis, [(i, i ^ bits) for i in range(size)])


def input_grad_kernel(block, place, *refs):
    hidden, inputs = refs[0:4], refs[4:12]
    weight, keep, send, hidden_out, inputs_out, hidden_f32, inputs_f32, total = refs[12:]
    z, chip, core = place[0], place[1], place[2]
    tokens = hidden[0].shape[0]
    half = tokens // 2
    hidden_f32[...] = jnp.zeros_like(hidden_f32)
    inputs_f32[...] = jnp.zeros_like(inputs_f32)
    for k in range(4):
        hidden_f32[z ^ k, 0:tokens, :] = hidden[k][...].astype(F32)
        own, other = inputs[2 * k][...].astype(F32), inputs[2 * k + 1][...].astype(F32)
        inputs_f32[chip ^ k, 0:half, :] = jnp.where(core == 0, own, other)
        inputs_f32[chip ^ k, half:tokens, :] = jnp.where(core == 0, other, own)
    hidden_out[...] = hidden_f32[...].reshape(hidden_out.shape).astype(BF16)
    inputs_out[...] = inputs_f32[...].reshape(inputs_out.shape).astype(BF16)

    def body(i, carry):
        rows = pl.multiple_of(i * block, block)
        total[:, pl.ds(rows, block)] = lax.dot_general(
            hidden_out[...], weight[pl.ds(rows, block), :], (((1,), (1,)), ((), ())), preferred_element_type=F32
        )
        return carry

    lax.fori_loop(0, weight.shape[0] // block, body, 0)
    for b in range(4):
        low = total[ROWS * b : ROWS * b + half, :]
        high = total[ROWS * b + half : ROWS * b + tokens, :]
        keep[b] = jnp.where(core == 0, low, high)
        send[b] = jnp.where(core == 0, high, low)


def input_grad_part(place, hidden, inputs, weight):
    depth, width = weight.shape
    half = inputs[0].shape[0]
    f = lambda shape, dtype: jax.ShapeDtypeStruct(shape, dtype)
    return pl.pallas_call(
        functools.partial(input_grad_kernel, 1024),
        in_specs=[SMEM] + [VMEM] * 13,
        out_specs=[VMEM] * 4,
        out_shape=[
            f((4, half, depth), F32),
            f((4, half, depth), F32),
            f((4 * ROWS, width), BF16),
            f((4 * ROWS, depth), BF16),
        ],
        scratch_shapes=[
            pltpu.VMEM((4, ROWS, width), F32),
            pltpu.VMEM((4, ROWS, depth), F32),
            pltpu.VMEM((4 * ROWS, depth), F32),
        ],
        compiler_params=pltpu.CompilerParams(vmem_limit_bytes=16 * MIB),
        name="input_grad_part",
    )(place, *hidden, *inputs, pltpu.with_memory_space_constraint(weight, pltpu.VMEM))


def weight_grad_kernel(first, count, block, inputs, hidden, *refs):
    out, buffer, sems = refs[-3:]

    def copy(i, slot):
        rows = pl.multiple_of((first + i) * block, block)
        return pltpu.make_async_copy(buffer.at[slot], out.at[pl.ds(rows, block), :], sems.at[slot])

    def body(i, carry):
        slot = lax.rem(i, 2)

        @pl.when(i >= 2)
        def _():
            copy(i - 2, slot).wait()

        rows = pl.multiple_of((first + i) * block, block)
        left = inputs[:, pl.ds(rows, block)]
        buffer[slot] = lax.dot_general(
            left, hidden[...], (((0,), (0,)), ((), ())), preferred_element_type=F32
        ).astype(BF16)
        copy(i, slot).start()
        return carry

    lax.fori_loop(0, count, body, 0)
    for i in range(max(0, count - 2), count):
        copy(i, i % 2).wait()


def weight_grad_part(first, count, block, inputs, hidden, before=None):
    shape = jax.ShapeDtypeStruct((inputs.shape[1], hidden.shape[1]), BF16)
    return pl.pallas_call(
        functools.partial(weight_grad_kernel, first, count, block),
        in_specs=[VMEM, VMEM] + ([] if before is None else [ANY]),
        out_specs=ANY,
        out_shape=shape,
        scratch_shapes=[pltpu.VMEM((2, block, shape.shape[1]), BF16), pltpu.SemaphoreType.DMA((2,))],
        input_output_aliases={} if before is None else {2: 0},
        compiler_params=pltpu.CompilerParams(vmem_limit_bytes=32 * MIB),
        name="weight_grad_part",
    )(inputs, hidden, *([] if before is None else [before]))


def fast(inputs, weight, out_grad, pre_act):
    z, m = lax.axis_index("batch"), lax.axis_index("mp")
    chip, core = m // 2, m % 2
    place = jnp.stack([z, chip, core]).astype(jnp.int32)
    own = gelu_back(pre_act, out_grad)
    hidden = [own] + [exchange(own, "batch", 4, k) for k in (1, 2, 3)]
    other = exchange(inputs, "mp", 8, 1)
    parts = [inputs, other]
    pair = jnp.stack([inputs, other])
    for k in (1, 2, 3):
        got = exchange(pair, "mp", 8, 2 * k)
        parts += [got[0], got[1]]
    keep, send, hidden, inputs = input_grad_part(place, hidden, parts, weight)

    got = exchange(send, "mp", 8, 1)
    block = 256
    blocks = inputs.shape[1] // block
    first = blocks // 3
    grad = weight_grad_part(0, first, block, inputs, hidden)
    mine = keep + got
    sends = [lax.dynamic_index_in_dim(mine, chip ^ k, 0, keepdims=False) for k in range(4)]
    gots = [exchange(sends[k], "mp", 8, 2 * k) for k in (1, 2, 3)]
    grad = weight_grad_part(first, blocks - first, block, inputs, hidden, grad)
    input_grad = (sends[0] + gots[0] + gots[1] + gots[2]).astype(BF16)
    return input_grad, grad


def plain(inputs, weight, out_grad, pre_act):
    hidden = lax.all_gather(gelu_back(pre_act, out_grad), "batch", axis=0, tiled=True)
    inputs = lax.all_gather(inputs, "mp", axis=0, tiled=True)
    weight_grad = lax.dot_general(
        inputs, hidden, (((0,), (0,)), ((), ())), preferred_element_type=F32
    ).astype(BF16)
    input_grad = lax.psum_scatter(
        lax.dot_general(hidden, weight, (((1,), (1,)), ((), ())), preferred_element_type=F32),
        "mp",
        scatter_dimension=0,
        tiled=True,
    ).astype(BF16)
    return input_grad, weight_grad


def solution(mesh):
    small = mesh.shape["batch"] == 4 and mesh.shape["mp"] == 8
    return jax.shard_map(
        fast if small else plain,
        mesh=mesh,
        in_specs=(P("mp", "batch"), P("batch", "mp"), P("batch", "mp"), P("batch", "mp")),
        out_specs=(P("mp", "batch"), P("batch", "mp")),
        check_vma=False,
    )
```

time: 153 us -> 66.7 us (0.44)
  blocking collectives: 67.1 us -> 0 us
  local copies, waits for them, and re-layouts: 50.7 us -> 12.6 us
  matrix products: 32 us -> 0 us
  Pallas kernels: 0 us -> 30.5 us
  starting transfers between devices: 0 us -> 14.2 us
  waiting for transfers between devices: 0 us -> 5.69 us
  other arithmetic: 0.4 us -> 2.63 us
    all_gather x3 -> x0, blocking collectives: 41.7 us -> none  [the longest x1 15.6 us: shards(): lax.all_gather(pre_act, 'batch', axis=0, tiled=True)]
    unnamed x3 -> x4, local copies, waits for them, and re-layouts: 49.9 us -> 12.5 us
    dot_general x2 -> x0, matrix products: 32 us -> none  [the longest x1 16.1 us: shards(): lax.dot_general(lax.all_gather(inputs, 'mp', axis=0, tiled=True), rows, (...]
    pallas_call x0 -> x3, Pallas kernels: none -> 30.5 us  [the longest x2 18.1 us: weight_grad_part(): pl.pallas_call(functools.partial(weight_grad_kernel, first, count, block)...]
    unnamed x1 -> x0, blocking collectives: 25.5 us -> none
    ppermute x0 -> x11, starting transfers between devices: none -> 14.2 us  [exchange(): return lax.ppermute(x, axis, [(i, i ^ bits) for i in range(size)])]
    ppermute x0 -> x11, waiting for transfers between devices: none -> 5.69 us  [exchange(): return lax.ppermute(x, axis, [(i, i ^ bits) for i in range(size)])]
  transfers between devices with their start and end apart: 0 -> 11, of which waited for: 0 -> 4; matrix products, arithmetic and copies ran while one was open for 0% -> 3% of each run, Pallas kernels for 0% -> 27%
where the time goes in v1:
time: 66.7 us; the launch traced here: 66.4 us
  Pallas kernels  30.5 us (46%)
  starting transfers between devices  14.2 us (21%)
  local copies, waits for them, and re-layouts  12.6 us (19%)
  waiting for transfers between devices  5.69 us (9%)
  other arithmetic  2.63 us (4%)
  between operations  0.77 us (1%)
    pallas_call x2, Pallas kernels, weight_grad_part(): pl.pallas_call(functools.partial(weight_grad_kernel, first, count, block)...  18.1 us
    ppermute x11, starting transfers between devices, exchange(): return lax.ppermute(x, axis, [(i, i ^ bits) for i in range(size)])  14.2 us
    unnamed x4, local copies, waits for them, and re-layouts  12.5 us
    pallas_call x1, Pallas kernels, input_grad_part(): pl.pallas_call(functools.partial(input_grad_kernel, 1024), in_specs=[SMEM...  12.3 us
    ppermute x11, waiting for transfers between devices, exchange(): return lax.ppermute(x, axis, [(i, i ^ bits) for i in range(size)])  5.69 us
  transfers between devices with their start and end apart: 11, of which 4 were waited for; matrix products, arithmetic and copies ran while one was open for 3% of the time, Pallas kernels for 27%

profile of v1, /device:TPU:0, one launch (start us, length us, event | category | flops | bytes accessed | tf_op | source)
XLA Modules:
  0.0 66.4 jit_solution(5559524086891472315)
XLA Ops:
  0.6 0.5 collective-permute-start.3
  1.1 1.1 %fusion.3.refs_0_ = bf16[6,6144]{1,0:T(8,128)(2,1)S(1)} fusion(bf16[6,6144]{1,0:T(8,128)(2,1)} %param.6, bf16[6,6144]{1,0:T(8,128)(2,1)} %param.7), kind=kLoop, calls=%fused_computation.8 | loop fusion | flops 811008 | bytes 221184 | tf_op jit(solution)/shard_map/convert_element_type | solution.py:22
  2.2 4.7 %collective-permute-start.2 = (bf16[6,6144]{1,0:T(8,128)(2,1)S(1)}, bf16[6,6144]{1,0:T(8,128)(2,1)S(1)}, u32[]{:S(2)}, u32[]{:S(2)}) collective-permute-start(bf16[6,6144]{1,0:T(8,128)(2,1)S(1)} %fusion.3.refs_0_), channel_id=1, source_target_pairs={{0,3},{1,2},{2,1},{3,0},{4,7},{5,6},{6,5},{7,4},{8,11},{9,10},{10,... | collective-permute-start | bytes 221192 | tf_op jit(solution)/shard_map/ppermute | solution.py:26
  6.9 0.0 collective-permute-start.1
  6.9 0.6 collective-permute-start
  7.6 0.0 collective-permute-done.3.refs_5_
  7.6 0.8 %pad_maximum_fusion = bf16[2,3,3072]{2,1,0:T(4,128)(2,1)S(1)} fusion(bf16[1,3,3072]{2,1,0:T(4,128)(2,1)S(1)} %bitcast.32, bf16[1,3,3072]{2,1,0:T(4,128)(2,1)} %bitcast.31), kind=kLoop, calls=%fused_computation.15 | loop fusion | flops 18432 | bytes 73728 | tf_op jit(solution)/shard_map/stack | solution.py:133
  8.3 2.7 %collective-permute-start.6 = (bf16[2,3,3072]{2,1,0:T(4,128)(2,1)S(1)}, bf16[2,3,3072]{2,1,0:T(4,128)(2,1)S(1)}, u32[]{:S(2)}, u32[]{:S(2)}) collective-permute-start(bf16[2,3,3072]{2,1,0:T(4,128)(2,1)S(1)} %pad_maximum_fusion), channel_id=1, source_target_pairs={{0,24},{4,28},{8,16},{12,20},{16,8},{20,12},{24,0},{28,4},{1,25},{... | collective-permute-start | bytes 110600 | tf_op jit(solution)/shard_map/ppermute | solution.py:26
  11.0 0.1 pad_add_fusion.place
  11.1 0.5 collective-permute-start.5
  11.6 1.8 %collective-permute-done.6 = bf16[2,3,3072]{2,1,0:T(4,128)(2,1)S(1)} collective-permute-done((bf16[2,3,3072]{2,1,0:T(4,128)(2,1)S(1)}, bf16[2,3,3072]{2,1,0:T(4,128)(2,1)S(1)}, u32[]{:S(2)}, u32[]{:S(2)}) %collective-permute-start.6) | collective-permute-done | bytes 36896 | tf_op jit(solution)/shard_map/ppermute | solution.py:26
  13.4 1.6 %collective-permute-start.4 = (bf16[2,3,3072]{2,1,0:T(4,128)(2,1)S(1)}, bf16[2,3,3072]{2,1,0:T(4,128)(2,1)S(1)}, u32[]{:S(2)}, u32[]{:S(2)}) collective-permute-start(bf16[2,3,3072]{2,1,0:T(4,128)(2,1)S(1)} %pad_maximum_fusion), channel_id=1, source_target_pairs={{0,8},{4,12},{8,0},{12,4},{16,24},{20,28},{24,16},{28,20},{1,9},{5... | collective-permute-start | bytes 110600 | tf_op jit(solution)/shard_map/ppermute | solution.py:26
  15.1 0.1 collective-permute-done.5
  15.2 2.3 %collective-permute-done.4 = bf16[2,3,3072]{2,1,0:T(4,128)(2,1)S(1)} collective-permute-done((bf16[2,3,3072]{2,1,0:T(4,128)(2,1)S(1)}, bf16[2,3,3072]{2,1,0:T(4,128)(2,1)S(1)}, u32[]{:S(2)}, u32[]{:S(2)}) %collective-permute-start.4) | collective-permute-done | bytes 36896 | tf_op jit(solution)/shard_map/ppermute | solution.py:26
  17.5 0.0 collective-permute-done.2.refs_3_
  17.5 0.0 collective-permute-done.1.refs_2_
  17.6 0.0 collective-permute-done.refs_1_
  17.6 0.0 copy-start
  17.6 11.7 %copy-done = bf16[3072,6144]{1,0:T(8,128)(2,1)S(1)} copy-done((bf16[3072,6144]{1,0:T(8,128)(2,1)S(1)}, bf16[3072,6144]{1,0:T(8,128)(2,1)}, u32[]{:S(2)}) %copy-start) | copy-done | bytes 37748760
  29.3 0.0 copy-start.1
  29.3 0.7 %copy-done.1 = bf16[3,3072]{1,0:T(4,128)(2,1)S(1)} copy-done((bf16[3,3072]{1,0:T(4,128)(2,1)S(1)}, bf16[3,3072]{1,0:T(4,128)(2,1)}, u32[]{:S(2)}) %copy-start.1) | copy-done | bytes 18456
  30.0 12.3 %input_grad_part.1 = (f32[4,3,3072]{2,1,0:T(4,128)S(1)}, f32[4,3,3072]{2,1,0:T(4,128)S(1)}, bf16[32,6144]{1,0:T(8,128)(2,1)S(1)}, bf16[32,3072]{1,0:T(8,128)(2,1)S(1)}) custom-call(s32[3]{0:T(128)S(1)} %pad_add_fusion.place, bf16[6,6144]{1,0:T(8,128)(2,1)S(1)} %fusion.3.refs_0_, bf16[6,6144]{1,0:T(8,128)(2,1)S(1)} %collective-permute-done.refs_1_, ...), custom_call_target="tpu_custom_call" | custom-call | tf_op jit(solution)/shard_map/input_grad_part/pallas_call | solution.py:64
  42.4 0.1 collective-permute-start.7
  42.5 1.4 %collective-permute-done.7 = f32[4,3,3072]{2,1,0:T(4,128)S(1)} collective-permute-done((f32[4,3,3072]{2,1,0:T(4,128)S(1)}, f32[4,3,3072]{2,1,0:T(4,128)S(1)}, u32[]{:S(2)}, u32[]{:S(2)}) %collective-permute-start.7) | collective-permute-done | bytes 147488 | tf_op jit(solution)/shard_map/ppermute | solution.py:26
  43.9 0.1 add.40
  44.0 1.7 %collective-permute-start.8 = (f32[3,3072]{1,0:T(4,128)S(1)}, f32[3,3072]{1,0:T(4,128)S(1)}, u32[]{:S(2)}, u32[]{:S(2)}) collective-permute-start(f32[3,3072]{1,0:T(4,128)S(1)} %get-tuple-element.10), channel_id=1, source_target_pairs={{0,8},{4,12},{8,0},{12,4},{16,24},{20,28},{24,16},{28,20},{1,9},{5... | collective-permute-start | bytes 110600 | tf_op jit(solution)/shard_map/ppermute | solution.py:26
  45.7 1.5 %collective-permute-start.10 = (f32[3,3072]{1,0:T(4,128)S(1)}, f32[3,3072]{1,0:T(4,128)S(1)}, u32[]{:S(2)}, u32[]{:S(2)}) collective-permute-start(f32[3,3072]{1,0:T(4,128)S(1)} %get-tuple-element.11), channel_id=1, source_target_pairs={{0,24},{4,28},{8,16},{12,20},{16,8},{20,12},{24,0},{28,4},{1,25},{... | collective-permute-start | bytes 110600 | tf_op jit(solution)/shard_map/ppermute | solution.py:26
  47.2 0.4 collective-permute-start.9
  47.6 6.4 %weight_grad_part.2.refs_0_ = bf16[3072,6144]{1,0:T(8,128)(2,1)} custom-call(bf16[32,3072]{1,0:T(8,128)(2,1)S(1)} %get-tuple-element.8.inputs, bf16[32,6144]{1,0:T(8,128)(2,1)S(1)} %get-tuple-element.9.hidden), custom_call_target="tpu_custom_call" | custom-call | tf_op jit(solution)/shard_map/weight_grad_part/pallas_call | solution.py:113
  54.0 11.7 %weight_grad_part.3 = bf16[3072,6144]{1,0:T(8,128)(2,1)} custom-call(bf16[32,3072]{1,0:T(8,128)(2,1)S(1)} %get-tuple-element.8.inputs, bf16[32,6144]{1,0:T(8,128)(2,1)S(1)} %get-tuple-element.9.hidden, bf16[3072,6144]{1,0:T(8,128)(2,1)} %weight_grad_part.2.refs_0_), custom_call_target="tpu_custom_call", output_to_operand_aliasing={{}: (2, {})} | custom-call | tf_op jit(solution)/shard_map/weight_grad_part/pallas_call | solution.py:113
  65.7 0.0 collective-permute-done.8
  65.7 0.0 collective-permute-done.10
  65.7 0.0 collective-permute-done.9
  65.7 0.6 fusion.12
  (4 shorter events, 0.1 us)
Async XLA Ops:
  0.6 6.9 %collective-permute-start.3 = (bf16[3,3072]{1,0:T(4,128)(2,1)}, bf16[3,3072]{1,0:T(4,128)(2,1)S(1)}, u32[]{:S(2)}, u32[]{:S(2)}) collective-permute-start(bf16[3,3072]{1,0:T(4,128)(2,1)} %refs_4_.1), channel_id=1, source_target_pairs={{0,4},{4,0},{8,12},{12,8},{16,20},{20,16},{24,28},{28,24},{1,5},{5... | collective-permute-start | bytes 55304 | tf_op jit(solution)/shard_map/ppermute | solution.py:26
  2.2 15.3 %collective-permute-start.2 = (bf16[6,6144]{1,0:T(8,128)(2,1)S(1)}, bf16[6,6144]{1,0:T(8,128)(2,1)S(1)}, u32[]{:S(2)}, u32[]{:S(2)}) collective-permute-start(bf16[6,6144]{1,0:T(8,128)(2,1)S(1)} %fusion.3.refs_0_), channel_id=1, source_target_pairs={{0,3},{1,2},{2,1},{3,0},{4,7},{5,6},{6,5},{7,4},{8,11},{9,10},{10,... | collective-permute-start | bytes 221192 | tf_op jit(solution)/shard_map/ppermute | solution.py:26
  6.9 10.6 %collective-permute-start.1 = (bf16[6,6144]{1,0:T(8,128)(2,1)S(1)}, bf16[6,6144]{1,0:T(8,128)(2,1)S(1)}, u32[]{:S(2)}, u32[]{:S(2)}) collective-permute-start(bf16[6,6144]{1,0:T(8,128)(2,1)S(1)} %fusion.3.refs_0_), channel_id=1, source_target_pairs={{0,2},{1,3},{2,0},{3,1},{4,6},{5,7},{6,4},{7,5},{8,10},{9,11},{10,... | collective-permute-start | bytes 221192 | tf_op jit(solution)/shard_map/ppermute | solution.py:26
  6.9 10.6 %collective-permute-start = (bf16[6,6144]{1,0:T(8,128)(2,1)S(1)}, bf16[6,6144]{1,0:T(8,128)(2,1)S(1)}, u32[]{:S(2)}, u32[]{:S(2)}) collective-permute-start(bf16[6,6144]{1,0:T(8,128)(2,1)S(1)} %fusion.3.refs_0_), channel_id=1, source_target_pairs={{0,1},{1,0},{2,3},{3,2},{4,5},{5,4},{6,7},{7,6},{8,9},{9,8},{10,11... | collective-permute-start | bytes 221192 | tf_op jit(solution)/shard_map/ppermute | solution.py:26
  8.3 5.1 %collective-permute-start.6 = (bf16[2,3,3072]{2,1,0:T(4,128)(2,1)S(1)}, bf16[2,3,3072]{2,1,0:T(4,128)(2,1)S(1)}, u32[]{:S(2)}, u32[]{:S(2)}) collective-permute-start(bf16[2,3,3072]{2,1,0:T(4,128)(2,1)S(1)} %pad_maximum_fusion), channel_id=1, source_target_pairs={{0,24},{4,28},{8,16},{12,20},{16,8},{20,12},{24,0},{28,4},{1,25},{... | collective-permute-start | bytes 110600 | tf_op jit(solution)/shard_map/ppermute | solution.py:26
  11.1 4.1 %collective-permute-start.5 = (bf16[2,3,3072]{2,1,0:T(4,128)(2,1)S(1)}, bf16[2,3,3072]{2,1,0:T(4,128)(2,1)S(1)}, u32[]{:S(2)}, u32[]{:S(2)}) collective-permute-start(bf16[2,3,3072]{2,1,0:T(4,128)(2,1)S(1)} %pad_maximum_fusion), channel_id=1, source_target_pairs={{0,16},{4,20},{8,24},{12,28},{16,0},{20,4},{24,8},{28,12},{1,17},{... | collective-permute-start | bytes 110600 | tf_op jit(solution)/shard_map/ppermute | solution.py:26
  13.4 4.1 %collective-permute-start.4 = (bf16[2,3,3072]{2,1,0:T(4,128)(2,1)S(1)}, bf16[2,3,3072]{2,1,0:T(4,128)(2,1)S(1)}, u32[]{:S(2)}, u32[]{:S(2)}) collective-permute-start(bf16[2,3,3072]{2,1,0:T(4,128)(2,1)S(1)} %pad_maximum_fusion), channel_id=1, source_target_pairs={{0,8},{4,12},{8,0},{12,4},{16,24},{20,28},{24,16},{28,20},{1,9},{5... | collective-permute-start | bytes 110600 | tf_op jit(solution)/shard_map/ppermute | solution.py:26
  17.6 11.7 %copy-start = (bf16[3072,6144]{1,0:T(8,128)(2,1)S(1)}, bf16[3072,6144]{1,0:T(8,128)(2,1)}, u32[]{:S(2)}) copy-start(bf16[3072,6144]{1,0:T(8,128)(2,1)} %refs_12_.1) | copy-start | bytes 113246208
  29.3 0.7 %copy-start.1 = (bf16[3,3072]{1,0:T(4,128)(2,1)S(1)}, bf16[3,3072]{1,0:T(4,128)(2,1)}, u32[]{:S(2)}) copy-start(bf16[3,3072]{1,0:T(4,128)(2,1)} %refs_4_.1) | copy-start | bytes 55300
  42.4 1.5 %collective-permute-start.7 = (f32[4,3,3072]{2,1,0:T(4,128)S(1)}, f32[4,3,3072]{2,1,0:T(4,128)S(1)}, u32[]{:S(2)}, u32[]{:S(2)}) collective-permute-start(f32[4,3,3072]{2,1,0:T(4,128)S(1)} %get-tuple-element.7), channel_id=1, source_target_pairs={{0,4},{4,0},{8,12},{12,8},{16,20},{20,16},{24,28},{28,24},{1,5},{5... | collective-permute-start | bytes 442376 | tf_op jit(solution)/shard_map/ppermute | solution.py:26
  44.0 21.7 %collective-permute-start.8 = (f32[3,3072]{1,0:T(4,128)S(1)}, f32[3,3072]{1,0:T(4,128)S(1)}, u32[]{:S(2)}, u32[]{:S(2)}) collective-permute-start(f32[3,3072]{1,0:T(4,128)S(1)} %get-tuple-element.10), channel_id=1, source_target_pairs={{0,8},{4,12},{8,0},{12,4},{16,24},{20,28},{24,16},{28,20},{1,9},{5... | collective-permute-start | bytes 110600 | tf_op jit(solution)/shard_map/ppermute | solution.py:26
  45.7 20.0 %collective-permute-start.10 = (f32[3,3072]{1,0:T(4,128)S(1)}, f32[3,3072]{1,0:T(4,128)S(1)}, u32[]{:S(2)}, u32[]{:S(2)}) collective-permute-start(f32[3,3072]{1,0:T(4,128)S(1)} %get-tuple-element.11), channel_id=1, source_target_pairs={{0,24},{4,28},{8,16},{12,20},{16,8},{20,12},{24,0},{28,4},{1,25},{... | collective-permute-start | bytes 110600 | tf_op jit(solution)/shard_map/ppermute | solution.py:26
  47.2 18.5 %collective-permute-start.9 = (f32[3,3072]{1,0:T(4,128)S(1)}, f32[3,3072]{1,0:T(4,128)S(1)}, u32[]{:S(2)}, u32[]{:S(2)}) collective-permute-start(f32[3,3072]{1,0:T(4,128)S(1)} %get-tuple-element.12), channel_id=1, source_target_pairs={{0,16},{4,20},{8,24},{12,28},{16,0},{20,4},{24,8},{28,12},{1,17},{... | collective-permute-start | bytes 110600 | tf_op jit(solution)/shard_map/ppermute | solution.py:26

commit v2 on v1

v2 whole, which is shorter than its diff:
```python
import functools

import jax
import jax.numpy as jnp
from jax import lax
from jax.experimental import pallas as pl
from jax.experimental.pallas import tpu as pltpu
from jax.sharding import PartitionSpec as P

F32, BF16 = jnp.float32, jnp.bfloat16
MIB = 1 << 20
MXU = 256
LANES = 128
ROWS = 8
VMEM = pl.BlockSpec(memory_space=pltpu.VMEM)
SMEM = pl.BlockSpec(memory_space=pltpu.SMEM)
ANY = pl.BlockSpec(memory_space=pl.ANY)


def gelu_back(pre_act, out_grad):
    value, pullback = jax.vjp(
        lambda v: jax.nn.gelu(v, approximate=True), pre_act.astype(F32)
    )
    return pullback(out_grad.astype(F32))[0].astype(BF16)


def in_hbm(x):
    return pltpu.with_memory_space_constraint(x, pltpu.HBM)


def hidden_kernel(pre_act, out_grad, inputs, own, inputs_out, pre, out, sems):
    pairs = ((pre_act, pre), (out_grad, out), (inputs, inputs_out))
    copies = [pltpu.make_async_copy(x, y, sems.at[i]) for i, (x, y) in enumerate(pairs)]
    for copy in copies:
        copy.start()
    for copy in copies:
        copy.wait()
    own[...] = gelu_back(pre[...], out[...])


def hidden_part(pre_act, out_grad, inputs):
    buffer = pltpu.VMEM(pre_act.shape, BF16)
    return pl.pallas_call(
        hidden_kernel,
        in_specs=[ANY] * 3,
        out_specs=[VMEM] * 2,
        out_shape=[buffer, pltpu.VMEM(inputs.shape, inputs.dtype)],
        scratch_shapes=[buffer, buffer, pltpu.SemaphoreType.DMA((3,))],
        compiler_params=pltpu.CompilerParams(vmem_limit_bytes=4 * MIB),
        name="hidden_part",
    )(*[in_hbm(x) for x in (pre_act, out_grad, inputs)])


def exchange(x, axis, size, bits):
    return lax.ppermute(x, axis, [(i, i ^ bits) for i in range(size)])


def gather_rows(place, pieces, padded):
    z, tokens = place[0], pieces[0].shape[0]
    padded[...] = jnp.zeros_like(padded)
    for k in range(4):
        padded[z ^ k, 0:tokens, :] = pieces[k][...].astype(F32)


def weight_rows(weight, tiles, sems, i):
    rows, slot = pl.ds(pl.multiple_of(i * MXU, MXU), MXU), i % tiles.shape[0]
    return pltpu.make_async_copy(weight.at[rows, :], tiles.at[slot], sems.at[slot])


def load_kernel(first, after, weight, tiles, sems):
    copies = [
        pltpu.make_async_copy(weight.at[pl.ds((first + i) * MXU, MXU), :], tiles.at[i], sems.at[i])
        for i in range(tiles.shape[0])
    ]
    for copy in copies:
        copy.start()
    for copy in copies:
        copy.wait()


def load_part(first, count, after, weight):
    return pl.pallas_call(
        functools.partial(load_kernel, first),
        in_specs=[ANY, ANY],
        out_specs=VMEM,
        out_shape=pltpu.VMEM((count, MXU, weight.shape[1]), weight.dtype),
        scratch_shapes=[pltpu.SemaphoreType.DMA((count,))],
        compiler_params=pltpu.CompilerParams(vmem_limit_bytes=2 * MIB),
        name="load_part",
    )(after, in_hbm(weight))


def both_kernel(shared, place, *refs):
    hidden, inputs, weight = refs[0:4], refs[4:8], refs[8]
    early, refs = refs[9], refs[10:]
    grad, hidden_out, inputs_out, keep, send = refs[0:5]
    hidden_f32, inputs_f32, turned, total, tiles, out, load_sems, out_sems = refs[5:]
    depth, width = weight.shape
    blocks, steps, ahead, tall = depth // MXU, width // MXU, tiles.shape[0] - 2, 2 * MXU
    ready = early.shape[0]

    for i in range(ready, min(ready + ahead, blocks)):
        weight_rows(weight, tiles, load_sems, i).start()
    gather_rows(place, hidden, hidden_f32)
    hidden_out[...] = hidden_f32[...].reshape(hidden_out.shape).astype(BF16)
    tokens = hidden[0].shape[0]
    half = tokens // 2
    chip, core = place[1], place[2]
    inputs_f32[...] = jnp.zeros_like(inputs_f32)
    for k in range(4):
        own, other = inputs[k][0].astype(F32), inputs[k][1].astype(F32)
        inputs_f32[chip ^ k, 0:half, :] = jnp.where(core == 0, own, other)
        inputs_f32[chip ^ k, half:tokens, :] = jnp.where(core == 0, other, own)
    inputs_out[...] = inputs_f32[...].reshape(inputs_out.shape).astype(BF16)

    def write(s, slot):
        return pltpu.make_async_copy(out.at[slot], grad.at[pl.ds(s * tall, tall), :], out_sems.at[slot])

    def scoped(*sums):
        small, large = (sums[0:2], sums[2:4]), (sums[4:6], sums[6:8])

        def superblock(s, with_grad):
            known = isinstance(s, int) and 2 * s < ready
            base = s * tall if isinstance(s, int) else pl.multiple_of(s * tall, tall)
            for a in () if known else (0, 1):
                i = 2 * s + a
                weight_rows(weight, tiles, load_sems, i).wait()

                @pl.when(i + ahead < blocks)
                def _():
                    weight_rows(weight, tiles, load_sems, i + ahead).start()

            def push_weight(m, k, a, stage):
                columns = slice(k * MXU, (k + 1) * MXU)
                tile = early[2 * s + a, :, columns] if known else tiles[(2 * s + a) % tiles.shape[0], :, columns]
                pltpu.matmul_push_rhs(tile, stage, m, transpose=True)

            def push_hidden(m, k, stage):
                tile = hidden_out[:, k * MXU : (k + 1) * MXU]
                blank = jnp.zeros((MXU - tile.shape[0], MXU), BF16)
                pltpu.matmul_push_rhs(jnp.concatenate([tile, blank], 0), stage, m)

            def times_weight(m, k, a, stage):
                left = hidden_out[:, k * MXU : (k + 1) * MXU]
                pltpu.matmul_acc_lhs(small[m][a], left, load_staged_rhs=stage)

            both = (0, 1)
            if with_grad:
                slot = s % out.shape[0]
                if s >= out.shape[0]:
                    write(s - out.shape[0], slot).wait()

                left = inputs_out[:, pl.ds(base, tall)]
                blank = jnp.zeros((turned.shape[1] - left.shape[0], tall), BF16)
                turned[...] = jnp.concatenate([left, blank], 0).T
                wide = jnp.zeros((MXU, MXU - turned.shape[1]), BF16)

                def times_hidden(m, a, stage):
                    left = jnp.concatenate([turned[a * MXU : (a + 1) * MXU, :], wide], 1)
                    pltpu.matmul_acc_lhs(large[m][a], left, load_staged_rhs=stage)

                def store(m, k, a):
                    out[slot, a * MXU : (a + 1) * MXU, k * MXU : (k + 1) * MXU] = pltpu.matmul_pop(
                        large[m][a]
                    ).astype(BF16)

                for m in both:
                    push_hidden(m, m, 0)
                for j in range(steps // 2):
                    h, o = j % 2, 1 - j % 2
                    for m in both:
                        times_hidden(m, 0, h)
                        push_weight(m, 2 * j + m, 0, o)
                    for m in both:
                        times_hidden(m, 1, None)
                        push_weight(m, 2 * j + m, 1, h)
                    for m in both:
                        store(m, 2 * j + m, 0)
                        times_weight(m, 2 * j + m, 0, o)
                        if 2 * j + 2 < steps:
                            push_hidden(m, 2 * j + 2 + m, o)
                        times_weight(m, 2 * j + m, 1, h)
                    for m in both:
                        store(m, 2 * j + m, 1)
                write(s, slot).start()
            else:
                for m in both:
                    push_weight(m, m, 0, 0)
                for j in range(steps // 2):
                    for m in both:
                        push_weight(m, 2 * j + m, 1, 1)
                        times_weight(m, 2 * j + m, 0, 0)
                    for m in both:
                        if 2 * j + 2 < steps:
                            push_weight(m, 2 * j + 2 + m, 0, 0)
                        times_weight(m, 2 * j + m, 1, 1)
            for a in (0, 1):
                rows = pl.ds(pl.multiple_of(base + a * MXU, MXU), MXU)
                total[:, rows] = pltpu.matmul_pop(small[0][a]) + pltpu.matmul_pop(small[1][a])

        def body(s, carry):
            superblock(s, False)
            return carry

        for s in range(shared):
            superblock(s, True)
        lax.fori_loop(shared, blocks // 2, body, 0)

    sums = [pltpu.ACC(m)((4 * ROWS, MXU), F32) for m in (0, 0, 1, 1)]
    sums += [pltpu.ACC(m)((MXU, MXU), F32) for m in (0, 0, 1, 1)]
    pl.run_scoped(scoped, *sums)
    for b in range(4):
        low = total[ROWS * b : ROWS * b + half, :]
        high = total[ROWS * b + half : ROWS * b + tokens, :]
        keep[b] = jnp.where(core == 0, low, high)
        send[b] = jnp.where(core == 0, high, low)
    for s in range(max(0, shared - out.shape[0]), shared):
        write(s, s % out.shape[0]).wait()


def both_part(shared, place, hidden, inputs, weight, early):
    depth, width = weight.shape
    half = hidden[0].shape[0] // 2
    f = lambda shape, dtype: jax.ShapeDtypeStruct(shape, dtype)
    slots, ahead = 2, 6
    return pl.pallas_call(
        functools.partial(both_kernel, shared),
        in_specs=[SMEM] + [VMEM] * 8 + [ANY, VMEM],
        out_specs=[ANY] + [VMEM] * 4,
        out_shape=[
            f((depth, width), BF16),
            f((4 * ROWS, width), BF16),
            f((4 * ROWS, depth), BF16),
            f((4, half, depth), F32),
            f((4, half, depth), F32),
        ],
        scratch_shapes=[
            pltpu.VMEM((4, ROWS, width), F32),
            pltpu.VMEM((4, ROWS, depth), F32),
            pltpu.VMEM((2 * MXU, LANES), BF16),
            pltpu.VMEM((4 * ROWS, depth), F32),
            pltpu.VMEM((ahead, MXU, width), BF16),
            pltpu.VMEM((slots, 2 * MXU, width), BF16),
            pltpu.SemaphoreType.DMA((ahead,)),
            pltpu.SemaphoreType.DMA((slots,)),
        ],
        compiler_params=pltpu.CompilerParams(vmem_limit_bytes=40 * MIB),
        name="both_part",
    )(place, *hidden, *inputs, in_hbm(weight), early)


def weight_grad_kernel(first, count, block, slots, inputs, hidden, *refs):
    out, buffer, sems = refs[-3:]

    def copy(i, slot):
        rows = pl.multiple_of((first + i) * block, block)
        return pltpu.make_async_copy(buffer.at[slot], out.at[pl.ds(rows, block), :], sems.at[slot])

    def body(i, carry):
        slot = lax.rem(i, slots)

        @pl.when(i >= slots)
        def _():
            copy(i - slots, slot).wait()

        rows = pl.multiple_of((first + i) * block, block)
        left = inputs[:, pl.ds(rows, block)]
        buffer[slot] = lax.dot_general(
            left, hidden[...], (((0,), (0,)), ((), ())), preferred_element_type=F32
        ).astype(BF16)
        copy(i, slot).start()
        return carry

    lax.fori_loop(0, count, body, 0)
    for i in range(max(0, count - slots), count):
        copy(i, i % slots).wait()


def weight_grad_part(first, count, inputs, hidden, before=None):
    shape = jax.ShapeDtypeStruct((inputs.shape[1], hidden.shape[1]), BF16)
    block, slots = MXU, 4
    return pl.pallas_call(
        functools.partial(weight_grad_kernel, first, count, block, slots),
        in_specs=[VMEM] * 2 + ([] if before is None else [ANY]),
        out_specs=ANY,
        out_shape=shape,
        scratch_shapes=[
            pltpu.VMEM((slots, block, shape.shape[1]), BF16),
            pltpu.SemaphoreType.DMA((slots,)),
        ],
        input_output_aliases={} if before is None else {2: 0},
        compiler_params=pltpu.CompilerParams(vmem_limit_bytes=20 * MIB),
        name="weight_grad_part",
    )(inputs, hidden, *([] if before is None else [before]))


def fast(inputs, weight, out_grad, pre_act):
    z, m = lax.axis_index("batch"), lax.axis_index("mp")
    chip, core = m // 2, m % 2
    place = jnp.stack([z, chip, core]).astype(jnp.int32)
    blocks, shared = weight.shape[0] // MXU, 3

    own, inputs = hidden_part(pre_act, out_grad, inputs)
    other = exchange(inputs, "mp", 8, 1)
    hidden = [own] + [exchange(own, "batch", 4, k) for k in (1, 2, 3)]
    pair = jnp.stack([inputs, other])
    late, hidden[1] = lax.optimization_barrier((pair, hidden[1]))
    pairs = [pair, exchange(pair, "mp", 8, 4), exchange(pair, "mp", 8, 2), exchange(late, "mp", 8, 6)]
    pairs = [pairs[0], pairs[2], pairs[1], pairs[3]]
    early = load_part(0, 4, late, weight)
    grad, hidden, inputs, keep, send = both_part(shared, place, hidden, pairs, weight, early)

    got = exchange(send, "mp", 8, 1)
    first, middle = 2 * shared, 2 * shared + 2
    grad = weight_grad_part(first, middle - first, inputs, hidden, grad)
    grad, keep = lax.optimization_barrier((grad, keep))
    mine = keep + got
    sends = [lax.dynamic_index_in_dim(mine, chip ^ k, 0, keepdims=False) for k in range(4)]
    gots = [exchange(sends[k], "mp", 8, 2 * k) for k in (1, 2, 3)]
    grad = weight_grad_part(middle, blocks - middle, inputs, hidden, grad)
    input_grad = (sends[0] + gots[0] + gots[1] + gots[2]).astype(BF16)
    return input_grad, grad


def plain(inputs, weight, out_grad, pre_act):
    hidden = lax.all_gather(gelu_back(pre_act, out_grad), "batch", axis=0, tiled=True)
    inputs = lax.all_gather(inputs, "mp", axis=0, tiled=True)
    weight_grad = lax.dot_general(
        inputs, hidden, (((0,), (0,)), ((), ())), preferred_element_type=F32
    ).astype(BF16)
    input_grad = lax.psum_scatter(
        lax.dot_general(hidden, weight, (((1,), (1,)), ((), ())), preferred_element_type=F32),
        "mp",
        scatter_dimension=0,
        tiled=True,
    ).astype(BF16)
    return input_grad, weight_grad


def solution(mesh):
    small = mesh.shape["batch"] == 4 and mesh.shape["mp"] == 8
    return jax.shard_map(
        fast if small else plain,
        mesh=mesh,
        in_specs=(P("mp", "batch"), P("batch", "mp"), P("batch", "mp"), P("batch", "mp")),
        out_specs=(P("mp", "batch"), P("batch", "mp")),
        check_vma=False,
    )
```

time: 66.7 us -> 49.3 us (0.74)
  local copies, waits for them, and re-layouts: 12.6 us -> 0.04 us
  waiting for transfers between devices: 5.69 us -> 0.03 us
  Pallas kernels: 30.5 us -> 34.5 us
  other arithmetic: 2.63 us -> 0.81 us
  starting transfers between devices: 14.2 us -> 12.9 us
    unnamed x4 -> x0, local copies, waits for them, and re-layouts: 12.5 us -> none
    ppermute x11, waiting for transfers between devices: 5.69 us -> 0.03 us  [exchange(): return lax.ppermute(x, axis, [(i, i ^ bits) for i in range(size)])]
    pallas_call x3 -> x5, Pallas kernels: 30.5 us -> 34.5 us  [the longest x1 19.2 us: both_part(): pl.pallas_call(functools.partial(both_kernel, shared), in_specs=[SMEM] +...]
    ppermute x11, starting transfers between devices: 14.2 us -> 12.9 us  [exchange(): return lax.ppermute(x, axis, [(i, i ^ bits) for i in range(size)])]
    convert_element_type x1 -> x0, other arithmetic: 1.09 us -> none  [gelu_back(): return pullback(out_grad.astype(F32))[0].astype(BF16)]
    another operation x1, other arithmetic: 0.77 us -> 0.04 us  [fast(): pair = jnp.stack([inputs, other])]
  transfers between devices with their start and end apart: 11 -> 11, of which waited for: 4 -> 0; matrix products, arithmetic and copies ran while one was open for 3% -> 0% of each run, Pallas kernels for 27% -> 29%
where the time goes in v2:
time: 49.3 us; the launch traced here: 49.1 us
  Pallas kernels  34.5 us (70%)
  starting transfers between devices  12.9 us (26%)
  other arithmetic  0.81 us (2%)
  between operations  0.79 us (2%)
    pallas_call x1, Pallas kernels, both_part(): pl.pallas_call(functools.partial(both_kernel, shared), in_specs=[SMEM] +...  19.2 us
    ppermute x11, starting transfers between devices, exchange(): return lax.ppermute(x, axis, [(i, i ^ bits) for i in range(size)])  12.9 us
    pallas_call x2, Pallas kernels, weight_grad_part(): pl.pallas_call(functools.partial(weight_grad_kernel, first, count, block,...  9.47 us
    pallas_call x1, Pallas kernels, load_part(): pl.pallas_call(functools.partial(load_kernel, first), in_specs=[ANY, ANY]...  4.69 us
    pallas_call x1, Pallas kernels, hidden_part(): pl.pallas_call(hidden_kernel, in_specs=[ANY] * 3, out_specs=[VMEM] * 2, o...  1.12 us
  transfers between devices with their start and end apart: 11, of which 0 were waited for; matrix products, arithmetic and copies ran while one was open for 0% of the time, Pallas kernels for 29%

profile of v2, /device:TPU:0, one launch (start us, length us, event | category | flops | bytes accessed | tf_op | source)
XLA Modules:
  0.0 49.1 jit_solution(4120471514080485720)
XLA Ops:
  0.6 1.1 %hidden_part.1 = (bf16[6,6144]{1,0:T(8,128)(2,1)S(1)}, bf16[3,3072]{1,0:T(4,128)(2,1)S(1)}) custom-call(bf16[6,6144]{1,0:T(8,128)(2,1)} %pre_act.1, bf16[6,6144]{1,0:T(8,128)(2,1)} %out_grad.1, bf16[3,3072]{1,0:T(4,128)(2,1)} %inputs.1), custom_call_target="tpu_custom_call" | custom-call | tf_op jit(solution)/shard_map/hidden_part/pallas_call | solution.py:43
  1.8 0.5 %collective-permute-start = (bf16[3,3072]{1,0:T(4,128)(2,1)S(1)}, bf16[3,3072]{1,0:T(4,128)(2,1)S(1)}, u32[]{:S(2)}, u32[]{:S(2)}) collective-permute-start(bf16[3,3072]{1,0:T(4,128)(2,1)S(1)} %get-tuple-element.14), channel_id=1, source_target_pairs={{0,4},{4,0},{8,12},{12,8},{16,20},{20,16},{24,28},{28,24},{1,5},{5... | collective-permute-start | bytes 55304 | tf_op jit(solution)/shard_map/ppermute | solution.py:55
  2.3 2.6 %collective-permute-start.1 = (bf16[6,6144]{1,0:T(8,128)(2,1)S(1)}, bf16[6,6144]{1,0:T(8,128)(2,1)S(1)}, u32[]{:S(2)}, u32[]{:S(2)}) collective-permute-start(bf16[6,6144]{1,0:T(8,128)(2,1)S(1)} %get-tuple-element.13.refs_0_), channel_id=1, source_target_pairs={{0,1},{1,0},{2,3},{3,2},{4,5},{5,4},{6,7},{7,6},{8,9},{9,8},{10,11... | collective-permute-start | bytes 221192 | tf_op jit(solution)/shard_map/ppermute | solution.py:55
  4.9 2.6 %collective-permute-start.2 = (bf16[6,6144]{1,0:T(8,128)(2,1)S(1)}, bf16[6,6144]{1,0:T(8,128)(2,1)S(1)}, u32[]{:S(2)}, u32[]{:S(2)}) collective-permute-start(bf16[6,6144]{1,0:T(8,128)(2,1)S(1)} %get-tuple-element.13.refs_0_), channel_id=1, source_target_pairs={{0,2},{1,3},{2,0},{3,1},{4,6},{5,7},{6,4},{7,5},{8,10},{9,11},{10,... | collective-permute-start | bytes 221192 | tf_op jit(solution)/shard_map/ppermute | solution.py:55
  7.5 0.0 collective-permute-start.3
  7.5 0.0 collective-permute-done
  7.6 1.8 %collective-permute-start.4 = (bf16[2,3,3072]{2,1,0:T(4,128)(2,1)S(1)}, bf16[2,3,3072]{2,1,0:T(4,128)(2,1)S(1)}, u32[]{:S(2)}, u32[]{:S(2)}) collective-permute-start(bf16[2,3,3072]{2,1,0:T(4,128)(2,1)S(1)} %pad_maximum_fusion.after.refs_4_), channel_id=1, source_target_pairs={{0,8},{4,12},{8,0},{12,4},{16,24},{20,28},{24,16},{28,20},{1,9},{5... | collective-permute-start | bytes 110600 | tf_op jit(solution)/shard_map/ppermute | solution.py:55
  9.3 1.5 %collective-permute-start.5 = (bf16[2,3,3072]{2,1,0:T(4,128)(2,1)S(1)}, bf16[2,3,3072]{2,1,0:T(4,128)(2,1)S(1)}, u32[]{:S(2)}, u32[]{:S(2)}) collective-permute-start(bf16[2,3,3072]{2,1,0:T(4,128)(2,1)S(1)} %pad_maximum_fusion.after.refs_4_), channel_id=1, source_target_pairs={{0,16},{4,20},{8,24},{12,28},{16,0},{20,4},{24,8},{28,12},{1,17},{... | collective-permute-start | bytes 110600 | tf_op jit(solution)/shard_map/ppermute | solution.py:55
  10.9 0.0 collective-permute-done.1.refs_1_
  10.9 0.3 collective-permute-start.6
  11.1 0.1 pad_add_fusion.place
  11.2 4.7 %load_part.1.refs_9_ = bf16[4,256,6144]{2,1,0:T(8,128)(2,1)S(1)} custom-call(bf16[2,3,3072]{2,1,0:T(4,128)(2,1)S(1)} %pad_maximum_fusion.after.refs_4_, bf16[3072,6144]{1,0:T(8,128)(2,1)} %refs_8_.1), custom_call_target="tpu_custom_call" | custom-call | tf_op jit(solution)/shard_map/load_part/pallas_call | solution.py:82
  15.9 0.0 collective-permute-done.4.refs_5_
  15.9 0.0 collective-permute-done.5.refs_6_
  15.9 0.0 collective-permute-done.2.refs_2_
  15.9 0.0 collective-permute-done.3.refs_3_
  15.9 0.0 collective-permute-done.6.refs_7_
  15.9 19.2 %both_part.1 = (bf16[3072,6144]{1,0:T(8,128)(2,1)}, bf16[32,6144]{1,0:T(8,128)(2,1)S(1)}, bf16[32,3072]{1,0:T(8,128)(2,1)S(1)}, f32[4,3,3072]{2,1,0:T(4,128)S(1)}, f32[4,3,3072]{2,1,0:T(4,128)S(1)}) custom-call(s32[3]{0:T(128)S(1)} %pad_add_fusion.place, bf16[6,6144]{1,0:T(8,128)(2,1)S(1)} %get-tuple-element.13.refs_0_, ...), custom_call_target="tpu_custom_call" | custom-call | tf_op jit(solution)/shard_map/both_part/pallas_call | solution.py:226
  35.2 0.1 collective-permute-start.7
  35.3 3.7 %weight_grad_part.2.refs_0_ = bf16[3072,6144]{1,0:T(8,128)(2,1)} custom-call(bf16[32,3072]{1,0:T(8,128)(2,1)S(1)} %get-tuple-element.17.inputs, bf16[32,6144]{1,0:T(8,128)(2,1)S(1)} %get-tuple-element.18.hidden, bf16[3072,6144]{1,0:T(8,128)(2,1)} %get-tuple-element.19.refs_0_), custom_call_target="tpu_custom_call", output_to_operand_aliasing={{}: (2, {})} | custom-call | tf_op jit(solution)/shard_map/weight_grad_part/pallas_call | solution.py:282
  39.0 0.0 collective-permute-done.7
  39.1 0.1 add.31
  39.2 2.7 %collective-permute-start.10 = (f32[3,3072]{1,0:T(4,128)S(1)}, f32[3,3072]{1,0:T(4,128)S(1)}, u32[]{:S(2)}, u32[]{:S(2)}) collective-permute-start(f32[3,3072]{1,0:T(4,128)S(1)} %get-tuple-element.25), channel_id=1, source_target_pairs={{0,24},{4,28},{8,16},{12,20},{16,8},{20,12},{24,0},{28,4},{1,25},{... | collective-permute-start | bytes 110600 | tf_op jit(solution)/shard_map/ppermute | solution.py:55
  41.9 0.5 %collective-permute-start.9 = (f32[3,3072]{1,0:T(4,128)S(1)}, f32[3,3072]{1,0:T(4,128)S(1)}, u32[]{:S(2)}, u32[]{:S(2)}) collective-permute-start(f32[3,3072]{1,0:T(4,128)S(1)} %get-tuple-element.26), channel_id=1, source_target_pairs={{0,16},{4,20},{8,24},{12,28},{16,0},{20,4},{24,8},{28,12},{1,17},{... | collective-permute-start | bytes 110600 | tf_op jit(solution)/shard_map/ppermute | solution.py:55
  42.4 0.3 collective-permute-start.8
  42.7 5.7 %weight_grad_part.3 = bf16[3072,6144]{1,0:T(8,128)(2,1)} custom-call(bf16[32,3072]{1,0:T(8,128)(2,1)S(1)} %get-tuple-element.17.inputs, bf16[32,6144]{1,0:T(8,128)(2,1)S(1)} %get-tuple-element.18.hidden, bf16[3072,6144]{1,0:T(8,128)(2,1)} %weight_grad_part.2.refs_0_), custom_call_target="tpu_custom_call", output_to_operand_aliasing={{}: (2, {})} | custom-call | tf_op jit(solution)/shard_map/weight_grad_part/pallas_call | solution.py:282
  48.5 0.0 collective-permute-done.10
  48.5 0.0 collective-permute-done.9
  48.5 0.0 collective-permute-done.8
  48.5 0.6 %fusion.2 = bf16[3,3072]{1,0:T(4,128)(2,1)} fusion(f32[3,3072]{1,0:T(4,128)S(1)} %collective-permute-done.10, f32[3,3072]{1,0:T(4,128)S(1)} %collective-permute-done.9, f32[3,3072]{1,0:T(4,128)S(1)} %collective-permute-done.8, f32[4,3,3072]{2,1,0:T(4,128)S(1)} %add.31, s32[]{:T(128)S(6)} %select_n.26), kind=kLoop, calls=%fused_computation.4 | loop fusion | flops 36864 | bytes 165892 | tf_op jit(solution)/shard_map/convert_element_type | solution.py:321
  (2 shorter events, 0.1 us)
Async XLA Ops:
  1.8 5.8 %collective-permute-start = (bf16[3,3072]{1,0:T(4,128)(2,1)S(1)}, bf16[3,3072]{1,0:T(4,128)(2,1)S(1)}, u32[]{:S(2)}, u32[]{:S(2)}) collective-permute-start(bf16[3,3072]{1,0:T(4,128)(2,1)S(1)} %get-tuple-element.14), channel_id=1, source_target_pairs={{0,4},{4,0},{8,12},{12,8},{16,20},{20,16},{24,28},{28,24},{1,5},{5... | collective-permute-start | bytes 55304 | tf_op jit(solution)/shard_map/ppermute | solution.py:55
  2.3 8.6 %collective-permute-start.1 = (bf16[6,6144]{1,0:T(8,128)(2,1)S(1)}, bf16[6,6144]{1,0:T(8,128)(2,1)S(1)}, u32[]{:S(2)}, u32[]{:S(2)}) collective-permute-start(bf16[6,6144]{1,0:T(8,128)(2,1)S(1)} %get-tuple-element.13.refs_0_), channel_id=1, source_target_pairs={{0,1},{1,0},{2,3},{3,2},{4,5},{5,4},{6,7},{7,6},{8,9},{9,8},{10,11... | collective-permute-start | bytes 221192 | tf_op jit(solution)/shard_map/ppermute | solution.py:55
  4.9 11.0 %collective-permute-start.2 = (bf16[6,6144]{1,0:T(8,128)(2,1)S(1)}, bf16[6,6144]{1,0:T(8,128)(2,1)S(1)}, u32[]{:S(2)}, u32[]{:S(2)}) collective-permute-start(bf16[6,6144]{1,0:T(8,128)(2,1)S(1)} %get-tuple-element.13.refs_0_), channel_id=1, source_target_pairs={{0,2},{1,3},{2,0},{3,1},{4,6},{5,7},{6,4},{7,5},{8,10},{9,11},{10,... | collective-permute-start | bytes 221192 | tf_op jit(solution)/shard_map/ppermute | solution.py:55
  7.5 8.4 %collective-permute-start.3 = (bf16[6,6144]{1,0:T(8,128)(2,1)S(1)}, bf16[6,6144]{1,0:T(8,128)(2,1)S(1)}, u32[]{:S(2)}, u32[]{:S(2)}) collective-permute-start(bf16[6,6144]{1,0:T(8,128)(2,1)S(1)} %get-tuple-element.13.refs_0_), channel_id=1, source_target_pairs={{0,3},{1,2},{2,1},{3,0},{4,7},{5,6},{6,5},{7,4},{8,11},{9,10},{10,... | collective-permute-start | bytes 221192 | tf_op jit(solution)/shard_map/ppermute | solution.py:55
  7.6 8.3 %collective-permute-start.4 = (bf16[2,3,3072]{2,1,0:T(4,128)(2,1)S(1)}, bf16[2,3,3072]{2,1,0:T(4,128)(2,1)S(1)}, u32[]{:S(2)}, u32[]{:S(2)}) collective-permute-start(bf16[2,3,3072]{2,1,0:T(4,128)(2,1)S(1)} %pad_maximum_fusion.after.refs_4_), channel_id=1, source_target_pairs={{0,8},{4,12},{8,0},{12,4},{16,24},{20,28},{24,16},{28,20},{1,9},{5... | collective-permute-start | bytes 110600 | tf_op jit(solution)/shard_map/ppermute | solution.py:55
  9.3 6.6 %collective-permute-start.5 = (bf16[2,3,3072]{2,1,0:T(4,128)(2,1)S(1)}, bf16[2,3,3072]{2,1,0:T(4,128)(2,1)S(1)}, u32[]{:S(2)}, u32[]{:S(2)}) collective-permute-start(bf16[2,3,3072]{2,1,0:T(4,128)(2,1)S(1)} %pad_maximum_fusion.after.refs_4_), channel_id=1, source_target_pairs={{0,16},{4,20},{8,24},{12,28},{16,0},{20,4},{24,8},{28,12},{1,17},{... | collective-permute-start | bytes 110600 | tf_op jit(solution)/shard_map/ppermute | solution.py:55
  10.9 5.1 %collective-permute-start.6 = (bf16[2,3,3072]{2,1,0:T(4,128)(2,1)S(1)}, bf16[2,3,3072]{2,1,0:T(4,128)(2,1)S(1)}, u32[]{:S(2)}, u32[]{:S(2)}) collective-permute-start(bf16[2,3,3072]{2,1,0:T(4,128)(2,1)S(1)} %pad_maximum_fusion.after.refs_4_), channel_id=1, source_target_pairs={{0,24},{4,28},{8,16},{12,20},{16,8},{20,12},{24,0},{28,4},{1,25},{... | collective-permute-start | bytes 110600 | tf_op jit(solution)/shard_map/ppermute | solution.py:55
  35.2 3.9 %collective-permute-start.7 = (f32[4,3,3072]{2,1,0:T(4,128)S(1)}, f32[4,3,3072]{2,1,0:T(4,128)S(1)}, u32[]{:S(2)}, u32[]{:S(2)}) collective-permute-start(f32[4,3,3072]{2,1,0:T(4,128)S(1)} %get-tuple-element.22), channel_id=1, source_target_pairs={{0,4},{4,0},{8,12},{12,8},{16,20},{20,16},{24,28},{28,24},{1,5},{5... | collective-permute-start | bytes 442376 | tf_op jit(solution)/shard_map/ppermute | solution.py:55
  39.2 9.3 %collective-permute-start.10 = (f32[3,3072]{1,0:T(4,128)S(1)}, f32[3,3072]{1,0:T(4,128)S(1)}, u32[]{:S(2)}, u32[]{:S(2)}) collective-permute-start(f32[3,3072]{1,0:T(4,128)S(1)} %get-tuple-element.25), channel_id=1, source_target_pairs={{0,24},{4,28},{8,16},{12,20},{16,8},{20,12},{24,0},{28,4},{1,25},{... | collective-permute-start | bytes 110600 | tf_op jit(solution)/shard_map/ppermute | solution.py:55
  41.9 6.6 %collective-permute-start.9 = (f32[3,3072]{1,0:T(4,128)S(1)}, f32[3,3072]{1,0:T(4,128)S(1)}, u32[]{:S(2)}, u32[]{:S(2)}) collective-permute-start(f32[3,3072]{1,0:T(4,128)S(1)} %get-tuple-element.26), channel_id=1, source_target_pairs={{0,16},{4,20},{8,24},{12,28},{16,0},{20,4},{24,8},{28,12},{1,17},{... | collective-permute-start | bytes 110600 | tf_op jit(solution)/shard_map/ppermute | solution.py:55
  42.4 6.1 %collective-permute-start.8 = (f32[3,3072]{1,0:T(4,128)S(1)}, f32[3,3072]{1,0:T(4,128)S(1)}, u32[]{:S(2)}, u32[]{:S(2)}) collective-permute-start(f32[3,3072]{1,0:T(4,128)S(1)} %get-tuple-element.24), channel_id=1, source_target_pairs={{0,8},{4,12},{8,0},{12,4},{16,24},{20,28},{24,16},{28,20},{1,9},{5... | collective-permute-start | bytes 110600 | tf_op jit(solution)/shard_map/ppermute | solution.py:55

commit v3 on v2

--- a/solution.py
+++ b/solution.py
@@ -62,8 +62,8 @@
         padded[z ^ k, 0:tokens, :] = pieces[k][...].astype(F32)
 
 
-def weight_rows(weight, tiles, sems, i):
-    rows, slot = pl.ds(pl.multiple_of(i * MXU, MXU), MXU), i % tiles.shape[0]
+def weight_rows(weight, tiles, sems, i, ready):
+    rows, slot = pl.ds(pl.multiple_of(i * MXU, MXU), MXU), (i - ready) % tiles.shape[0]
     return pltpu.make_async_copy(weight.at[rows, :], tiles.at[slot], sems.at[slot])
 
 
@@ -90,17 +90,17 @@
     )(after, in_hbm(weight))
 
 
-def both_kernel(shared, place, *refs):
+def both_kernel(place, *refs):
     hidden, inputs, weight = refs[0:4], refs[4:8], refs[8]
     early, refs = refs[9], refs[10:]
     grad, hidden_out, inputs_out, keep, send = refs[0:5]
     hidden_f32, inputs_f32, turned, total, tiles, out, load_sems, out_sems = refs[5:]
     depth, width = weight.shape
-    blocks, steps, ahead, tall = depth // MXU, width // MXU, tiles.shape[0] - 2, 2 * MXU
-    ready = early.shape[0]
-
-    for i in range(ready, min(ready + ahead, blocks)):
-        weight_rows(weight, tiles, load_sems, i).start()
+    blocks, steps, tall = depth // MXU, width // MXU, 2 * MXU
+    ready, ring = early.shape[0], tiles.shape[0]
+
+    for i in range(ready, min(ready + ring, blocks)):
+        weight_rows(weight, tiles, load_sems, i, ready).start()
     gather_rows(place, hidden, hidden_f32)
     hidden_out[...] = hidden_f32[...].reshape(hidden_out.shape).astype(BF16)
     tokens = hidden[0].shape[0]
@@ -113,8 +113,11 @@
         inputs_f32[chip ^ k, half:tokens, :] = jnp.where(core == 0, other, own)
     inputs_out[...] = inputs_f32[...].reshape(inputs_out.shape).astype(BF16)
 
-    def write(s, slot):
-        return pltpu.make_async_copy(out.at[slot], grad.at[pl.ds(s * tall, tall), :], out_sems.at[slot])
+    slots, pairs = out.shape[0], blocks // 4
+
+    def write(p):
+        rows = pl.ds(pl.multiple_of(2 * p * tall, tall), tall)
+        return pltpu.make_async_copy(out.at[p % slots], grad.at[rows, :], out_sems.at[p % slots])
 
     def scoped(*sums):
         small, large = (sums[0:2], sums[2:4]), (sums[4:6], sums[6:8])
@@ -123,16 +126,16 @@
             known = isinstance(s, int) and 2 * s < ready
             base = s * tall if isinstance(s, int) else pl.multiple_of(s * tall, tall)
             for a in () if known else (0, 1):
-                i = 2 * s + a
-                weight_rows(weight, tiles, load_sems, i).wait()
-
-                @pl.when(i + ahead < blocks)
+                weight_rows(weight, tiles, load_sems, 2 * s + a, ready).wait()
+                free = 2 * s - 2 + a
+
+                @pl.when((free >= ready) & (free + ring < blocks))
                 def _():
-                    weight_rows(weight, tiles, load_sems, i + ahead).start()
+                    weight_rows(weight, tiles, load_sems, free + ring, ready).start()
 
             def push_weight(m, k, a, stage):
                 columns = slice(k * MXU, (k + 1) * MXU)
-                tile = early[2 * s + a, :, columns] if known else tiles[(2 * s + a) % tiles.shape[0], :, columns]
+                tile = early[2 * s + a, :, columns] if known else tiles[(2 * s + a - ready) % ring, :, columns]
                 pltpu.matmul_push_rhs(tile, stage, m, transpose=True)
 
             def push_hidden(m, k, stage):
@@ -146,9 +149,11 @@
 
             both = (0, 1)
             if with_grad:
-                slot = s % out.shape[0]
-                if s >= out.shape[0]:
-                    write(s - out.shape[0], slot).wait()
+                p = s // 2
+
+                @pl.when(p >= slots)
+                def _():
+                    write(p - slots).wait()
 
                 left = inputs_out[:, pl.ds(base, tall)]
                 blank = jnp.zeros((turned.shape[1] - left.shape[0], tall), BF16)
@@ -160,7 +165,7 @@
                     pltpu.matmul_acc_lhs(large[m][a], left, load_staged_rhs=stage)
 
                 def store(m, k, a):
-                    out[slot, a * MXU : (a + 1) * MXU, k * MXU : (k + 1) * MXU] = pltpu.matmul_pop(
+                    out[p % slots, a * MXU : (a + 1) * MXU, k * MXU : (k + 1) * MXU] = pltpu.matmul_pop(
                         large[m][a]
                     ).astype(BF16)
 
@@ -182,7 +187,7 @@
                         times_weight(m, 2 * j + m, 1, h)
                     for m in both:
                         store(m, 2 * j + m, 1)
-                write(s, slot).start()
+                write(p).start()
             else:
                 for m in both:
                     push_weight(m, m, 0, 0)
@@ -198,13 +203,14 @@
                 rows = pl.ds(pl.multiple_of(base + a * MXU, MXU), MXU)
                 total[:, rows] = pltpu.matmul_pop(small[0][a]) + pltpu.matmul_pop(small[1][a])
 
-        def body(s, carry):
-            superblock(s, False)
+        def body(p, carry):
+            superblock(2 * p, True)
+            superblock(2 * p + 1, False)
             return carry
 
-        for s in range(shared):
-            superblock(s, True)
-        lax.fori_loop(shared, blocks // 2, body, 0)
+        for p in range(ready // 4):
+            body(p, 0)
+        lax.fori_loop(ready // 4, pairs, body, 0)
 
     sums = [pltpu.ACC(m)((4 * ROWS, MXU), F32) for m in (0, 0, 1, 1)]
     sums += [pltpu.ACC(m)((MXU, MXU), F32) for m in (0, 0, 1, 1)]
@@ -214,17 +220,17 @@
         high = total[ROWS * b + half : ROWS * b + tokens, :]
         keep[b] = jnp.where(core == 0, low, high)
         send[b] = jnp.where(core == 0, high, low)
-    for s in range(max(0, shared - out.shape[0]), shared):
-        write(s, s % out.shape[0]).wait()
-
-
-def both_part(shared, place, hidden, inputs, weight, early):
+    for p in range(max(0, pairs - slots), pairs):
+        write(p).wait()
+
+
+def both_part(place, hidden, inputs, weight, early):
     depth, width = weight.shape
     half = hidden[0].shape[0] // 2
     f = lambda shape, dtype: jax.ShapeDtypeStruct(shape, dtype)
-    slots, ahead = 2, 6
+    slots, later = 2, 7
     return pl.pallas_call(
-        functools.partial(both_kernel, shared),
+        both_kernel,
         in_specs=[SMEM] + [VMEM] * 8 + [ANY, VMEM],
         out_specs=[ANY] + [VMEM] * 4,
         out_shape=[
@@ -239,9 +245,9 @@
             pltpu.VMEM((4, ROWS, depth), F32),
             pltpu.VMEM((2 * MXU, LANES), BF16),
             pltpu.VMEM((4 * ROWS, depth), F32),
-            pltpu.VMEM((ahead, MXU, width), BF16),
+            pltpu.VMEM((later, MXU, width), BF16),
             pltpu.VMEM((slots, 2 * MXU, width), BF16),
-            pltpu.SemaphoreType.DMA((ahead,)),
+            pltpu.SemaphoreType.DMA((later,)),
             pltpu.SemaphoreType.DMA((slots,)),
         ],
         compiler_params=pltpu.CompilerParams(vmem_limit_bytes=40 * MIB),
@@ -249,56 +255,67 @@
     )(place, *hidden, *inputs, in_hbm(weight), early)
 
 
-def weight_grad_kernel(first, count, block, slots, inputs, hidden, *refs):
+def weight_grad_kernel(first, count, block, slots, pieces, inputs, hidden, *refs):
     out, buffer, sems = refs[-3:]
-
-    def copy(i, slot):
-        rows = pl.multiple_of((first + i) * block, block)
-        return pltpu.make_async_copy(buffer.at[slot], out.at[pl.ds(rows, block), :], sems.at[slot])
+    width = out.shape[1] // pieces
+
+    def place(i):
+        i = first + i
+        return pl.multiple_of((4 * (i // 2) + 2 + i % 2) * block, block)
+
+    def copy(i, piece):
+        rows, columns = pl.ds(place(i), block), pl.ds(piece * width, width)
+        slot = i % slots
+        return pltpu.make_async_copy(
+            buffer.at[slot, :, columns], out.at[rows, columns], sems.at[slot, piece]
+        )
 
     def body(i, carry):
-        slot = lax.rem(i, slots)
+        slot = i % slots
 
         @pl.when(i >= slots)
         def _():
-            copy(i - slots, slot).wait()
-
-        rows = pl.multiple_of((first + i) * block, block)
-        left = inputs[:, pl.ds(rows, block)]
-        buffer[slot] = lax.dot_general(
-            left, hidden[...], (((0,), (0,)), ((), ())), preferred_element_type=F32
-        ).astype(BF16)
-        copy(i, slot).start()
+            for piece in range(pieces):
+                copy(i - slots, piece).wait()
+
+        left = inputs[:, pl.ds(place(i), block)]
+        for piece in range(pieces):
+            columns = slice(piece * width, (piece + 1) * width)
+            buffer[slot, :, columns] = lax.dot_general(
+                left, hidden[:, columns], (((0,), (0,)), ((), ())), preferred_element_type=F32
+            ).astype(BF16)
+            copy(i, piece).start()
         return carry
 
     lax.fori_loop(0, count, body, 0)
     for i in range(max(0, count - slots), count):
-        copy(i, i % slots).wait()
-
-
-def weight_grad_part(first, count, inputs, hidden, before=None):
-    shape = jax.ShapeDtypeStruct((inputs.shape[1], hidden.shape[1]), BF16)
-    block, slots = MXU, 4
+        for piece in range(pieces):
+            copy(i, piece).wait()
+
+
+def weight_grad_part(first, count, inputs, hidden, before):
+    shape = jax.ShapeDtypeStruct(before.shape, BF16)
+    block, slots, pieces = MXU, min(count, 4), 4
     return pl.pallas_call(
-        functools.partial(weight_grad_kernel, first, count, block, slots),
-        in_specs=[VMEM] * 2 + ([] if before is None else [ANY]),
+        functools.partial(weight_grad_kernel, first, count, block, slots, pieces),
+        in_specs=[VMEM, VMEM, ANY],
         out_specs=ANY,
         out_shape=shape,
         scratch_shapes=[
             pltpu.VMEM((slots, block, shape.shape[1]), BF16),
-            pltpu.SemaphoreType.DMA((slots,)),
+            pltpu.SemaphoreType.DMA((slots, pieces)),
         ],
-        input_output_aliases={} if before is None else {2: 0},
+        input_output_aliases={2: 0},
         compiler_params=pltpu.CompilerParams(vmem_limit_bytes=20 * MIB),
         name="weight_grad_part",
-    )(inputs, hidden, *([] if before is None else [before]))
+    )(inputs, hidden, before)
 
 
 def fast(inputs, weight, out_grad, pre_act):
     z, m = lax.axis_index("batch"), lax.axis_index("mp")
     chip, core = m // 2, m % 2
     place = jnp.stack([z, chip, core]).astype(jnp.int32)
-    blocks, shared = weight.shape[0] // MXU, 3
+    blocks = weight.shape[0] // (2 * MXU)
 
     own, inputs = hidden_part(pre_act, out_grad, inputs)
     other = exchange(inputs, "mp", 8, 1)
@@ -308,16 +325,16 @@
     pairs = [pair, exchange(pair, "mp", 8, 4), exchange(pair, "mp", 8, 2), exchange(late, "mp", 8, 6)]
     pairs = [pairs[0], pairs[2], pairs[1], pairs[3]]
     early = load_part(0, 4, late, weight)
-    grad, hidden, inputs, keep, send = both_part(shared, place, hidden, pairs, weight, early)
+    grad, hidden, inputs, keep, send = both_part(place, hidden, pairs, weight, early)
 
     got = exchange(send, "mp", 8, 1)
-    first, middle = 2 * shared, 2 * shared + 2
-    grad = weight_grad_part(first, middle - first, inputs, hidden, grad)
+    first = 1
+    grad = weight_grad_part(0, first, inputs, hidden, grad)
     grad, keep = lax.optimization_barrier((grad, keep))
     mine = keep + got
     sends = [lax.dynamic_index_in_dim(mine, chip ^ k, 0, keepdims=False) for k in range(4)]
     gots = [exchange(sends[k], "mp", 8, 2 * k) for k in (1, 2, 3)]
-    grad = weight_grad_part(middle, blocks - middle, inputs, hidden, grad)
+    grad = weight_grad_part(first, blocks - first, inputs, hidden, grad)
     input_grad = (sends[0] + gots[0] + gots[1] + gots[2]).astype(BF16)
     return input_grad, grad
 

time: 49.3 us -> 45.6 us (0.925)
  Pallas kernels: 34.5 us -> 30.9 us
    pallas_call x1, Pallas kernels: 19.2 us -> 16.8 us  [both_part(): pl.pallas_call(both_kernel, in_specs=[SMEM] + [VMEM] * 8 + [ANY, VMEM], o...]
    pallas_call x2, Pallas kernels: 9.47 us -> 8.28 us  [weight_grad_part(): pl.pallas_call(functools.partial(weight_grad_kernel, first, count, block,...]
  transfers between devices with their start and end apart: 11 -> 11, of which waited for: 0 -> 0; matrix products, arithmetic and copies ran while one was open for 0% -> 0% of each run, Pallas kernels for 29% -> 28%
where the time goes in v3:
time: 45.6 us; the launch traced here: 45.5 us
  Pallas kernels  30.9 us (68%)
  starting transfers between devices  12.9 us (28%)
  other arithmetic  0.81 us (2%)
  between operations  0.79 us (2%)
    pallas_call x1, Pallas kernels, both_part(): pl.pallas_call(both_kernel, in_specs=[SMEM] + [VMEM] * 8 + [ANY, VMEM], o...  16.8 us
    ppermute x11, starting transfers between devices, exchange(): return lax.ppermute(x, axis, [(i, i ^ bits) for i in range(size)])  12.9 us
    pallas_call x2, Pallas kernels, weight_grad_part(): pl.pallas_call(functools.partial(weight_grad_kernel, first, count, block,...  8.28 us
    pallas_call x1, Pallas kernels, load_part(): pl.pallas_call(functools.partial(load_kernel, first), in_specs=[ANY, ANY]...  4.69 us
    pallas_call x1, Pallas kernels, hidden_part(): pl.pallas_call(hidden_kernel, in_specs=[ANY] * 3, out_specs=[VMEM] * 2, o...  1.12 us
  transfers between devices with their start and end apart: 11, of which 0 were waited for; matrix products, arithmetic and copies ran while one was open for 0% of the time, Pallas kernels for 28%

profile of v3, /device:TPU:0, one launch (start us, length us, event | category | flops | bytes accessed | tf_op | source)
XLA Modules:
  0.0 45.5 jit_solution(1860517556419424301)
XLA Ops:
  0.6 1.1 %hidden_part.1 = (bf16[6,6144]{1,0:T(8,128)(2,1)S(1)}, bf16[3,3072]{1,0:T(4,128)(2,1)S(1)}) custom-call(bf16[6,6144]{1,0:T(8,128)(2,1)} %pre_act.1, bf16[6,6144]{1,0:T(8,128)(2,1)} %out_grad.1, bf16[3,3072]{1,0:T(4,128)(2,1)} %inputs.1), custom_call_target="tpu_custom_call" | custom-call | tf_op jit(solution)/shard_map/hidden_part/pallas_call | solution.py:43
  1.8 0.5 %collective-permute-start = (bf16[3,3072]{1,0:T(4,128)(2,1)S(1)}, bf16[3,3072]{1,0:T(4,128)(2,1)S(1)}, u32[]{:S(2)}, u32[]{:S(2)}) collective-permute-start(bf16[3,3072]{1,0:T(4,128)(2,1)S(1)} %get-tuple-element.14), channel_id=1, source_target_pairs={{0,4},{4,0},{8,12},{12,8},{16,20},{20,16},{24,28},{28,24},{1,5},{5... | collective-permute-start | bytes 55304 | tf_op jit(solution)/shard_map/ppermute | solution.py:55
  2.3 2.6 %collective-permute-start.1 = (bf16[6,6144]{1,0:T(8,128)(2,1)S(1)}, bf16[6,6144]{1,0:T(8,128)(2,1)S(1)}, u32[]{:S(2)}, u32[]{:S(2)}) collective-permute-start(bf16[6,6144]{1,0:T(8,128)(2,1)S(1)} %get-tuple-element.13.refs_0_), channel_id=1, source_target_pairs={{0,1},{1,0},{2,3},{3,2},{4,5},{5,4},{6,7},{7,6},{8,9},{9,8},{10,11... | collective-permute-start | bytes 221192 | tf_op jit(solution)/shard_map/ppermute | solution.py:55
  4.9 2.6 %collective-permute-start.2 = (bf16[6,6144]{1,0:T(8,128)(2,1)S(1)}, bf16[6,6144]{1,0:T(8,128)(2,1)S(1)}, u32[]{:S(2)}, u32[]{:S(2)}) collective-permute-start(bf16[6,6144]{1,0:T(8,128)(2,1)S(1)} %get-tuple-element.13.refs_0_), channel_id=1, source_target_pairs={{0,2},{1,3},{2,0},{3,1},{4,6},{5,7},{6,4},{7,5},{8,10},{9,11},{10,... | collective-permute-start | bytes 221192 | tf_op jit(solution)/shard_map/ppermute | solution.py:55
  7.5 0.0 collective-permute-start.3
  7.5 0.0 collective-permute-done
  7.6 1.8 %collective-permute-start.4 = (bf16[2,3,3072]{2,1,0:T(4,128)(2,1)S(1)}, bf16[2,3,3072]{2,1,0:T(4,128)(2,1)S(1)}, u32[]{:S(2)}, u32[]{:S(2)}) collective-permute-start(bf16[2,3,3072]{2,1,0:T(4,128)(2,1)S(1)} %pad_maximum_fusion.after.refs_4_), channel_id=1, source_target_pairs={{0,8},{4,12},{8,0},{12,4},{16,24},{20,28},{24,16},{28,20},{1,9},{5... | collective-permute-start | bytes 110600 | tf_op jit(solution)/shard_map/ppermute | solution.py:55
  9.3 1.5 %collective-permute-start.5 = (bf16[2,3,3072]{2,1,0:T(4,128)(2,1)S(1)}, bf16[2,3,3072]{2,1,0:T(4,128)(2,1)S(1)}, u32[]{:S(2)}, u32[]{:S(2)}) collective-permute-start(bf16[2,3,3072]{2,1,0:T(4,128)(2,1)S(1)} %pad_maximum_fusion.after.refs_4_), channel_id=1, source_target_pairs={{0,16},{4,20},{8,24},{12,28},{16,0},{20,4},{24,8},{28,12},{1,17},{... | collective-permute-start | bytes 110600 | tf_op jit(solution)/shard_map/ppermute | solution.py:55
  10.9 0.0 collective-permute-done.1.refs_1_
  10.9 0.3 collective-permute-start.6
  11.1 0.1 pad_add_fusion.place
  11.2 4.7 %load_part.1.refs_9_ = bf16[4,256,6144]{2,1,0:T(8,128)(2,1)S(1)} custom-call(bf16[2,3,3072]{2,1,0:T(4,128)(2,1)S(1)} %pad_maximum_fusion.after.refs_4_, bf16[3072,6144]{1,0:T(8,128)(2,1)} %refs_8_.1), custom_call_target="tpu_custom_call" | custom-call | tf_op jit(solution)/shard_map/load_part/pallas_call | solution.py:82
  15.9 0.0 collective-permute-done.4.refs_5_
  15.9 0.0 collective-permute-done.5.refs_6_
  15.9 0.0 collective-permute-done.2.refs_2_
  15.9 0.0 collective-permute-done.3.refs_3_
  15.9 0.0 collective-permute-done.6.refs_7_
  15.9 16.8 %both_part.1 = (bf16[3072,6144]{1,0:T(8,128)(2,1)}, bf16[32,6144]{1,0:T(8,128)(2,1)S(1)}, bf16[32,3072]{1,0:T(8,128)(2,1)S(1)}, f32[4,3,3072]{2,1,0:T(4,128)S(1)}, f32[4,3,3072]{2,1,0:T(4,128)S(1)}) custom-call(s32[3]{0:T(128)S(1)} %pad_add_fusion.place, bf16[6,6144]{1,0:T(8,128)(2,1)S(1)} %get-tuple-element.13.refs_0_, ...), custom_call_target="tpu_custom_call" | custom-call | tf_op jit(solution)/shard_map/both_part/pallas_call | solution.py:232
  32.8 0.1 collective-permute-start.7
  32.9 2.1 %weight_grad_part.2.refs_0_ = bf16[3072,6144]{1,0:T(8,128)(2,1)} custom-call(bf16[32,3072]{1,0:T(8,128)(2,1)S(1)} %get-tuple-element.17.inputs, bf16[32,6144]{1,0:T(8,128)(2,1)S(1)} %get-tuple-element.18.hidden, bf16[3072,6144]{1,0:T(8,128)(2,1)} %get-tuple-element.19.refs_0_), custom_call_target="tpu_custom_call", output_to_operand_aliasing={{}: (2, {})} | custom-call | tf_op jit(solution)/shard_map/weight_grad_part/pallas_call | solution.py:299
  34.9 0.0 collective-permute-done.7
  35.0 0.1 add.31
  35.1 2.7 %collective-permute-start.10 = (f32[3,3072]{1,0:T(4,128)S(1)}, f32[3,3072]{1,0:T(4,128)S(1)}, u32[]{:S(2)}, u32[]{:S(2)}) collective-permute-start(f32[3,3072]{1,0:T(4,128)S(1)} %get-tuple-element.25), channel_id=1, source_target_pairs={{0,24},{4,28},{8,16},{12,20},{16,8},{20,12},{24,0},{28,4},{1,25},{... | collective-permute-start | bytes 110600 | tf_op jit(solution)/shard_map/ppermute | solution.py:55
  37.8 0.5 %collective-permute-start.9 = (f32[3,3072]{1,0:T(4,128)S(1)}, f32[3,3072]{1,0:T(4,128)S(1)}, u32[]{:S(2)}, u32[]{:S(2)}) collective-permute-start(f32[3,3072]{1,0:T(4,128)S(1)} %get-tuple-element.26), channel_id=1, source_target_pairs={{0,16},{4,20},{8,24},{12,28},{16,0},{20,4},{24,8},{28,12},{1,17},{... | collective-permute-start | bytes 110600 | tf_op jit(solution)/shard_map/ppermute | solution.py:55
  38.3 0.3 collective-permute-start.8
  38.6 6.2 %weight_grad_part.3 = bf16[3072,6144]{1,0:T(8,128)(2,1)} custom-call(bf16[32,3072]{1,0:T(8,128)(2,1)S(1)} %get-tuple-element.17.inputs, bf16[32,6144]{1,0:T(8,128)(2,1)S(1)} %get-tuple-element.18.hidden, bf16[3072,6144]{1,0:T(8,128)(2,1)} %weight_grad_part.2.refs_0_), custom_call_target="tpu_custom_call", output_to_operand_aliasing={{}: (2, {})} | custom-call | tf_op jit(solution)/shard_map/weight_grad_part/pallas_call | solution.py:299
  44.8 0.0 collective-permute-done.10
  44.8 0.0 collective-permute-done.9
  44.8 0.0 collective-permute-done.8
  44.8 0.6 %fusion.2 = bf16[3,3072]{1,0:T(4,128)(2,1)} fusion(f32[3,3072]{1,0:T(4,128)S(1)} %collective-permute-done.10, f32[3,3072]{1,0:T(4,128)S(1)} %collective-permute-done.9, f32[3,3072]{1,0:T(4,128)S(1)} %collective-permute-done.8, f32[4,3,3072]{2,1,0:T(4,128)S(1)} %add.31, s32[]{:T(128)S(6)} %select_n.26), kind=kLoop, calls=%fused_computation.4 | loop fusion | flops 36864 | bytes 165892 | tf_op jit(solution)/shard_map/convert_element_type | solution.py:338
  (2 shorter events, 0.1 us)
Async XLA Ops:
  1.8 5.8 %collective-permute-start = (bf16[3,3072]{1,0:T(4,128)(2,1)S(1)}, bf16[3,3072]{1,0:T(4,128)(2,1)S(1)}, u32[]{:S(2)}, u32[]{:S(2)}) collective-permute-start(bf16[3,3072]{1,0:T(4,128)(2,1)S(1)} %get-tuple-element.14), channel_id=1, source_target_pairs={{0,4},{4,0},{8,12},{12,8},{16,20},{20,16},{24,28},{28,24},{1,5},{5... | collective-permute-start | bytes 55304 | tf_op jit(solution)/shard_map/ppermute | solution.py:55
  2.3 8.6 %collective-permute-start.1 = (bf16[6,6144]{1,0:T(8,128)(2,1)S(1)}, bf16[6,6144]{1,0:T(8,128)(2,1)S(1)}, u32[]{:S(2)}, u32[]{:S(2)}) collective-permute-start(bf16[6,6144]{1,0:T(8,128)(2,1)S(1)} %get-tuple-element.13.refs_0_), channel_id=1, source_target_pairs={{0,1},{1,0},{2,3},{3,2},{4,5},{5,4},{6,7},{7,6},{8,9},{9,8},{10,11... | collective-permute-start | bytes 221192 | tf_op jit(solution)/shard_map/ppermute | solution.py:55
  4.9 11.0 %collective-permute-start.2 = (bf16[6,6144]{1,0:T(8,128)(2,1)S(1)}, bf16[6,6144]{1,0:T(8,128)(2,1)S(1)}, u32[]{:S(2)}, u32[]{:S(2)}) collective-permute-start(bf16[6,6144]{1,0:T(8,128)(2,1)S(1)} %get-tuple-element.13.refs_0_), channel_id=1, source_target_pairs={{0,2},{1,3},{2,0},{3,1},{4,6},{5,7},{6,4},{7,5},{8,10},{9,11},{10,... | collective-permute-start | bytes 221192 | tf_op jit(solution)/shard_map/ppermute | solution.py:55
  7.5 8.4 %collective-permute-start.3 = (bf16[6,6144]{1,0:T(8,128)(2,1)S(1)}, bf16[6,6144]{1,0:T(8,128)(2,1)S(1)}, u32[]{:S(2)}, u32[]{:S(2)}) collective-permute-start(bf16[6,6144]{1,0:T(8,128)(2,1)S(1)} %get-tuple-element.13.refs_0_), channel_id=1, source_target_pairs={{0,3},{1,2},{2,1},{3,0},{4,7},{5,6},{6,5},{7,4},{8,11},{9,10},{10,... | collective-permute-start | bytes 221192 | tf_op jit(solution)/shard_map/ppermute | solution.py:55
  7.6 8.3 %collective-permute-start.4 = (bf16[2,3,3072]{2,1,0:T(4,128)(2,1)S(1)}, bf16[2,3,3072]{2,1,0:T(4,128)(2,1)S(1)}, u32[]{:S(2)}, u32[]{:S(2)}) collective-permute-start(bf16[2,3,3072]{2,1,0:T(4,128)(2,1)S(1)} %pad_maximum_fusion.after.refs_4_), channel_id=1, source_target_pairs={{0,8},{4,12},{8,0},{12,4},{16,24},{20,28},{24,16},{28,20},{1,9},{5... | collective-permute-start | bytes 110600 | tf_op jit(solution)/shard_map/ppermute | solution.py:55
  9.3 6.6 %collective-permute-start.5 = (bf16[2,3,3072]{2,1,0:T(4,128)(2,1)S(1)}, bf16[2,3,3072]{2,1,0:T(4,128)(2,1)S(1)}, u32[]{:S(2)}, u32[]{:S(2)}) collective-permute-start(bf16[2,3,3072]{2,1,0:T(4,128)(2,1)S(1)} %pad_maximum_fusion.after.refs_4_), channel_id=1, source_target_pairs={{0,16},{4,20},{8,24},{12,28},{16,0},{20,4},{24,8},{28,12},{1,17},{... | collective-permute-start | bytes 110600 | tf_op jit(solution)/shard_map/ppermute | solution.py:55
  10.9 5.1 %collective-permute-start.6 = (bf16[2,3,3072]{2,1,0:T(4,128)(2,1)S(1)}, bf16[2,3,3072]{2,1,0:T(4,128)(2,1)S(1)}, u32[]{:S(2)}, u32[]{:S(2)}) collective-permute-start(bf16[2,3,3072]{2,1,0:T(4,128)(2,1)S(1)} %pad_maximum_fusion.after.refs_4_), channel_id=1, source_target_pairs={{0,24},{4,28},{8,16},{12,20},{16,8},{20,12},{24,0},{28,4},{1,25},{... | collective-permute-start | bytes 110600 | tf_op jit(solution)/shard_map/ppermute | solution.py:55
  32.8 2.2 %collective-permute-start.7 = (f32[4,3,3072]{2,1,0:T(4,128)S(1)}, f32[4,3,3072]{2,1,0:T(4,128)S(1)}, u32[]{:S(2)}, u32[]{:S(2)}) collective-permute-start(f32[4,3,3072]{2,1,0:T(4,128)S(1)} %get-tuple-element.22), channel_id=1, source_target_pairs={{0,4},{4,0},{8,12},{12,8},{16,20},{20,16},{24,28},{28,24},{1,5},{5... | collective-permute-start | bytes 442376 | tf_op jit(solution)/shard_map/ppermute | solution.py:55
  35.1 9.8 %collective-permute-start.10 = (f32[3,3072]{1,0:T(4,128)S(1)}, f32[3,3072]{1,0:T(4,128)S(1)}, u32[]{:S(2)}, u32[]{:S(2)}) collective-permute-start(f32[3,3072]{1,0:T(4,128)S(1)} %get-tuple-element.25), channel_id=1, source_target_pairs={{0,24},{4,28},{8,16},{12,20},{16,8},{20,12},{24,0},{28,4},{1,25},{... | collective-permute-start | bytes 110600 | tf_op jit(solution)/shard_map/ppermute | solution.py:55
  37.8 7.0 %collective-permute-start.9 = (f32[3,3072]{1,0:T(4,128)S(1)}, f32[3,3072]{1,0:T(4,128)S(1)}, u32[]{:S(2)}, u32[]{:S(2)}) collective-permute-start(f32[3,3072]{1,0:T(4,128)S(1)} %get-tuple-element.26), channel_id=1, source_target_pairs={{0,16},{4,20},{8,24},{12,28},{16,0},{20,4},{24,8},{28,12},{1,17},{... | collective-permute-start | bytes 110600 | tf_op jit(solution)/shard_map/ppermute | solution.py:55
  38.3 6.5 %collective-permute-start.8 = (f32[3,3072]{1,0:T(4,128)S(1)}, f32[3,3072]{1,0:T(4,128)S(1)}, u32[]{:S(2)}, u32[]{:S(2)}) collective-permute-start(f32[3,3072]{1,0:T(4,128)S(1)} %get-tuple-element.24), channel_id=1, source_target_pairs={{0,8},{4,12},{8,0},{12,4},{16,24},{20,28},{24,16},{28,20},{1,9},{5... | collective-permute-start | bytes 110600 | tf_op jit(solution)/shard_map/ppermute | solution.py:55

commit v4 on v3

--- a/solution.py
+++ b/solution.py
@@ -13,7 +13,6 @@
 LANES = 128
 ROWS = 8
 VMEM = pl.BlockSpec(memory_space=pltpu.VMEM)
-SMEM = pl.BlockSpec(memory_space=pltpu.SMEM)
 ANY = pl.BlockSpec(memory_space=pl.ANY)
 
 
@@ -55,8 +54,8 @@
     return lax.ppermute(x, axis, [(i, i ^ bits) for i in range(size)])
 
 
-def gather_rows(place, pieces, padded):
-    z, tokens = place[0], pieces[0].shape[0]
+def gather_rows(z, pieces, padded):
+    tokens = pieces[0].shape[0]
     padded[...] = jnp.zeros_like(padded)
     for k in range(4):
         padded[z ^ k, 0:tokens, :] = pieces[k][...].astype(F32)
@@ -90,8 +89,10 @@
     )(after, in_hbm(weight))
 
 
-def both_kernel(place, *refs):
-    hidden, inputs, weight = refs[0:4], refs[4:8], refs[8]
+def both_kernel(*refs):
+    z, m = lax.axis_index("batch"), lax.axis_index("mp")
+    chip, core = m // 2, m % 2
+    hidden, inputs, weight = refs[3::-1], refs[4:8], refs[8]
     early, refs = refs[9], refs[10:]
     grad, hidden_out, inputs_out, keep, send = refs[0:5]
     hidden_f32, inputs_f32, turned, total, tiles, out, load_sems, out_sems = refs[5:]
@@ -101,11 +102,10 @@
 
     for i in range(ready, min(ready + ring, blocks)):
         weight_rows(weight, tiles, load_sems, i, ready).start()
-    gather_rows(place, hidden, hidden_f32)
+    gather_rows(z, hidden, hidden_f32)
     hidden_out[...] = hidden_f32[...].reshape(hidden_out.shape).astype(BF16)
     tokens = hidden[0].shape[0]
     half = tokens // 2
-    chip, core = place[1], place[2]
     inputs_f32[...] = jnp.zeros_like(inputs_f32)
     for k in range(4):
         own, other = inputs[k][0].astype(F32), inputs[k][1].astype(F32)
@@ -215,23 +215,23 @@
     sums = [pltpu.ACC(m)((4 * ROWS, MXU), F32) for m in (0, 0, 1, 1)]
     sums += [pltpu.ACC(m)((MXU, MXU), F32) for m in (0, 0, 1, 1)]
     pl.run_scoped(scoped, *sums)
-    for b in range(4):
-        low = total[ROWS * b : ROWS * b + half, :]
-        high = total[ROWS * b + half : ROWS * b + tokens, :]
-        keep[b] = jnp.where(core == 0, low, high)
-        send[b] = jnp.where(core == 0, high, low)
+    for k in range(4):
+        rows = total[pl.ds(pl.multiple_of(ROWS * (chip ^ k), ROWS), ROWS), :]
+        low, high = rows[:half], rows[half:tokens]
+        keep[k] = jnp.where(core == 0, low, high)
+        send[k] = jnp.where(core == 0, high, low)
     for p in range(max(0, pairs - slots), pairs):
         write(p).wait()
 
 
-def both_part(place, hidden, inputs, weight, early):
+def both_part(hidden, inputs, weight, early):
     depth, width = weight.shape
     half = hidden[0].shape[0] // 2
     f = lambda shape, dtype: jax.ShapeDtypeStruct(shape, dtype)
     slots, later = 2, 7
     return pl.pallas_call(
         both_kernel,
-        in_specs=[SMEM] + [VMEM] * 8 + [ANY, VMEM],
+        in_specs=[VMEM] * 8 + [ANY, VMEM],
         out_specs=[ANY] + [VMEM] * 4,
         out_shape=[
             f((depth, width), BF16),
@@ -252,7 +252,7 @@
         ],
         compiler_params=pltpu.CompilerParams(vmem_limit_bytes=40 * MIB),
         name="both_part",
-    )(place, *hidden, *inputs, in_hbm(weight), early)
+    )(*hidden[::-1], *inputs, in_hbm(weight), early)
 
 
 def weight_grad_kernel(first, count, block, slots, pieces, inputs, hidden, *refs):
@@ -312,9 +312,6 @@
 
 
 def fast(inputs, weight, out_grad, pre_act):
-    z, m = lax.axis_index("batch"), lax.axis_index("mp")
-    chip, core = m // 2, m % 2
-    place = jnp.stack([z, chip, core]).astype(jnp.int32)
     blocks = weight.shape[0] // (2 * MXU)
 
     own, inputs = hidden_part(pre_act, out_grad, inputs)
@@ -325,14 +322,14 @@
     pairs = [pair, exchange(pair, "mp", 8, 4), exchange(pair, "mp", 8, 2), exchange(late, "mp", 8, 6)]
     pairs = [pairs[0], pairs[2], pairs[1], pairs[3]]
     early = load_part(0, 4, late, weight)
-    grad, hidden, inputs, keep, send = both_part(place, hidden, pairs, weight, early)
+    grad, hidden, inputs, keep, send = both_part(hidden, pairs, weight, early)
 
     got = exchange(send, "mp", 8, 1)
     first = 1
     grad = weight_grad_part(0, first, inputs, hidden, grad)
     grad, keep = lax.optimization_barrier((grad, keep))
     mine = keep + got
-    sends = [lax.dynamic_index_in_dim(mine, chip ^ k, 0, keepdims=False) for k in range(4)]
+    sends = [mine[k] for k in range(4)]
     gots = [exchange(sends[k], "mp", 8, 2 * k) for k in (1, 2, 3)]
     grad = weight_grad_part(first, blocks - first, inputs, hidden, grad)
     input_grad = (sends[0] + gots[0] + gots[1] + gots[2]).astype(BF16)

time: 45.6 us -> 45.2 us (level)
  transfers between devices with their start and end apart: 11 -> 11, of which waited for: 0 -> 0; matrix products, arithmetic and copies ran while one was open for 0% -> 0% of each run, Pallas kernels for 28% -> 29%
where the time goes in v4:
time: 45.2 us; the launch traced here: 45 us
  Pallas kernels  30.5 us (67%)
  starting transfers between devices  12.9 us (29%)
  between operations  0.77 us (2%)
  other arithmetic  0.73 us (2%)
    pallas_call x1, Pallas kernels, both_part(): pl.pallas_call(both_kernel, in_specs=[VMEM] * 8 + [ANY, VMEM], out_specs=...  16.4 us
    ppermute x11, starting transfers between devices, exchange(): return lax.ppermute(x, axis, [(i, i ^ bits) for i in range(size)])  12.9 us
    pallas_call x2, Pallas kernels, weight_grad_part(): pl.pallas_call(functools.partial(weight_grad_kernel, first, count, block,...  8.28 us
    pallas_call x1, Pallas kernels, load_part(): pl.pallas_call(functools.partial(load_kernel, first), in_specs=[ANY, ANY]...  4.68 us
    pallas_call x1, Pallas kernels, hidden_part(): pl.pallas_call(hidden_kernel, in_specs=[ANY] * 3, out_specs=[VMEM] * 2, o...  1.12 us
  transfers between devices with their start and end apart: 11, of which 0 were waited for; matrix products, arithmetic and copies ran while one was open for 0% of the time, Pallas kernels for 29%

profile of v4, /device:TPU:0, one launch (start us, length us, event | category | flops | bytes accessed | tf_op | source)
XLA Modules:
  0.0 45.0 jit_solution(8049873413221280062)
XLA Ops:
  0.6 1.1 %hidden_part.1 = (bf16[6,6144]{1,0:T(8,128)(2,1)S(1)}, bf16[3,3072]{1,0:T(4,128)(2,1)S(1)}) custom-call(bf16[6,6144]{1,0:T(8,128)(2,1)} %pre_act.1, bf16[6,6144]{1,0:T(8,128)(2,1)} %out_grad.1, bf16[3,3072]{1,0:T(4,128)(2,1)} %inputs.1), custom_call_target="tpu_custom_call" | custom-call | tf_op jit(solution)/shard_map/hidden_part/pallas_call | solution.py:42
  1.8 0.5 %collective-permute-start.2 = (bf16[3,3072]{1,0:T(4,128)(2,1)S(1)}, bf16[3,3072]{1,0:T(4,128)(2,1)S(1)}, u32[]{:S(2)}, u32[]{:S(2)}) collective-permute-start(bf16[3,3072]{1,0:T(4,128)(2,1)S(1)} %get-tuple-element.14), channel_id=1, source_target_pairs={{0,4},{4,0},{8,12},{12,8},{16,20},{20,16},{24,28},{28,24},{1,5},{5... | collective-permute-start | bytes 55304 | tf_op jit(solution)/shard_map/ppermute | solution.py:54
  2.3 2.6 %collective-permute-start.3 = (bf16[6,6144]{1,0:T(8,128)(2,1)S(1)}, bf16[6,6144]{1,0:T(8,128)(2,1)S(1)}, u32[]{:S(2)}, u32[]{:S(2)}) collective-permute-start(bf16[6,6144]{1,0:T(8,128)(2,1)S(1)} %get-tuple-element.13.refs_3_), channel_id=1, source_target_pairs={{0,1},{1,0},{2,3},{3,2},{4,5},{5,4},{6,7},{7,6},{8,9},{9,8},{10,11... | collective-permute-start | bytes 221192 | tf_op jit(solution)/shard_map/ppermute | solution.py:54
  4.9 2.6 %collective-permute-start.1 = (bf16[6,6144]{1,0:T(8,128)(2,1)S(1)}, bf16[6,6144]{1,0:T(8,128)(2,1)S(1)}, u32[]{:S(2)}, u32[]{:S(2)}) collective-permute-start(bf16[6,6144]{1,0:T(8,128)(2,1)S(1)} %get-tuple-element.13.refs_3_), channel_id=1, source_target_pairs={{0,2},{1,3},{2,0},{3,1},{4,6},{5,7},{6,4},{7,5},{8,10},{9,11},{10,... | collective-permute-start | bytes 221192 | tf_op jit(solution)/shard_map/ppermute | solution.py:54
  7.5 0.0 collective-permute-start
  7.5 0.0 collective-permute-done.2
  7.6 1.8 %collective-permute-start.5 = (bf16[2,3,3072]{2,1,0:T(4,128)(2,1)S(1)}, bf16[2,3,3072]{2,1,0:T(4,128)(2,1)S(1)}, u32[]{:S(2)}, u32[]{:S(2)}) collective-permute-start(bf16[2,3,3072]{2,1,0:T(4,128)(2,1)S(1)} %pad_maximum_fusion.after.refs_4_), channel_id=1, source_target_pairs={{0,16},{4,20},{8,24},{12,28},{16,0},{20,4},{24,8},{28,12},{1,17},{... | collective-permute-start | bytes 110600 | tf_op jit(solution)/shard_map/ppermute | solution.py:54
  9.4 1.5 %collective-permute-start.4 = (bf16[2,3,3072]{2,1,0:T(4,128)(2,1)S(1)}, bf16[2,3,3072]{2,1,0:T(4,128)(2,1)S(1)}, u32[]{:S(2)}, u32[]{:S(2)}) collective-permute-start(bf16[2,3,3072]{2,1,0:T(4,128)(2,1)S(1)} %pad_maximum_fusion.after.refs_4_), channel_id=1, source_target_pairs={{0,8},{4,12},{8,0},{12,4},{16,24},{20,28},{24,16},{28,20},{1,9},{5... | collective-permute-start | bytes 110600 | tf_op jit(solution)/shard_map/ppermute | solution.py:54
  10.9 0.0 collective-permute-done.3.refs_2_
  10.9 0.3 collective-permute-start.6
  11.1 4.7 %load_part.1.refs_9_ = bf16[4,256,6144]{2,1,0:T(8,128)(2,1)S(1)} custom-call(bf16[2,3,3072]{2,1,0:T(4,128)(2,1)S(1)} %pad_maximum_fusion.after.refs_4_, bf16[3072,6144]{1,0:T(8,128)(2,1)} %refs_8_.1), custom_call_target="tpu_custom_call" | custom-call | tf_op jit(solution)/shard_map/load_part/pallas_call | solution.py:81
  15.8 0.0 collective-permute-done.5.refs_6_
  15.8 0.0 collective-permute-done.4.refs_5_
  15.8 0.0 collective-permute-done.1.refs_1_
  15.8 0.0 collective-permute-done.refs_0_
  15.9 0.0 collective-permute-done.6.refs_7_
  15.9 16.4 %both_part.1 = (bf16[3072,6144]{1,0:T(8,128)(2,1)}, bf16[32,6144]{1,0:T(8,128)(2,1)S(1)}, bf16[32,3072]{1,0:T(8,128)(2,1)S(1)}, f32[4,3,3072]{2,1,0:T(4,128)S(1)}, f32[4,3,3072]{2,1,0:T(4,128)S(1)}) custom-call(bf16[6,6144]{1,0:T(8,128)(2,1)S(1)} %collective-permute-done.refs_0_, bf16[6,6144]{1,0:T(8,128)(2,1)S(1)} %collective-permute-done.1.refs_1_, ...), custom_call_target="tpu_custom_call" | custom-call | tf_op jit(solution)/shard_map/both_part/pallas_call | solution.py:232
  32.3 0.1 collective-permute-start.7
  32.4 2.1 %weight_grad_part.2.refs_0_ = bf16[3072,6144]{1,0:T(8,128)(2,1)} custom-call(bf16[32,3072]{1,0:T(8,128)(2,1)S(1)} %get-tuple-element.17.inputs, bf16[32,6144]{1,0:T(8,128)(2,1)S(1)} %get-tuple-element.18.hidden, bf16[3072,6144]{1,0:T(8,128)(2,1)} %get-tuple-element.19.refs_0_), custom_call_target="tpu_custom_call", output_to_operand_aliasing={{}: (2, {})} | custom-call | tf_op jit(solution)/shard_map/weight_grad_part/pallas_call | solution.py:299
  34.5 0.0 collective-permute-done.7
  34.5 0.1 add.12
  34.6 1.8 %collective-permute-start.8 = (f32[3,3072]{1,0:T(4,128)S(1)}, f32[3,3072]{1,0:T(4,128)S(1)}, u32[]{:S(2)}, u32[]{:S(2)}) collective-permute-start(f32[3,3072]{1,0:T(4,128)S(1)} %get-tuple-element.24), channel_id=1, source_target_pairs={{0,8},{4,12},{8,0},{12,4},{16,24},{20,28},{24,16},{28,20},{1,9},{5... | collective-permute-start | bytes 110600 | tf_op jit(solution)/shard_map/ppermute | solution.py:54
  36.4 1.5 %collective-permute-start.10 = (f32[3,3072]{1,0:T(4,128)S(1)}, f32[3,3072]{1,0:T(4,128)S(1)}, u32[]{:S(2)}, u32[]{:S(2)}) collective-permute-start(f32[3,3072]{1,0:T(4,128)S(1)} %get-tuple-element.25), channel_id=1, source_target_pairs={{0,24},{4,28},{8,16},{12,20},{16,8},{20,12},{24,0},{28,4},{1,25},{... | collective-permute-start | bytes 110600 | tf_op jit(solution)/shard_map/ppermute | solution.py:54
  37.9 0.3 collective-permute-start.9
  38.1 6.2 %weight_grad_part.3 = bf16[3072,6144]{1,0:T(8,128)(2,1)} custom-call(bf16[32,3072]{1,0:T(8,128)(2,1)S(1)} %get-tuple-element.17.inputs, bf16[32,6144]{1,0:T(8,128)(2,1)S(1)} %get-tuple-element.18.hidden, bf16[3072,6144]{1,0:T(8,128)(2,1)} %weight_grad_part.2.refs_0_), custom_call_target="tpu_custom_call", output_to_operand_aliasing={{}: (2, {})} | custom-call | tf_op jit(solution)/shard_map/weight_grad_part/pallas_call | solution.py:299
  44.3 0.0 collective-permute-done.8
  44.4 0.0 collective-permute-done.10
  44.4 0.0 collective-permute-done.9
  44.4 0.6 %fusion.3 = bf16[3,3072]{1,0:T(4,128)(2,1)} fusion(f32[3,3072]{1,0:T(4,128)S(1)} %collective-permute-done.10, f32[3,3072]{1,0:T(4,128)S(1)} %collective-permute-done.9, f32[3,3072]{1,0:T(4,128)S(1)} %collective-permute-done.8, f32[4,3,3072]{2,1,0:T(4,128)S(1)} %add.12), kind=kLoop, calls=%fused_computation.7 | loop fusion | flops 36864 | bytes 165888 | tf_op jit(solution)/shard_map/convert_element_type | solution.py:335
  (2 shorter events, 0.1 us)
Async XLA Ops:
  1.8 5.8 %collective-permute-start.2 = (bf16[3,3072]{1,0:T(4,128)(2,1)S(1)}, bf16[3,3072]{1,0:T(4,128)(2,1)S(1)}, u32[]{:S(2)}, u32[]{:S(2)}) collective-permute-start(bf16[3,3072]{1,0:T(4,128)(2,1)S(1)} %get-tuple-element.14), channel_id=1, source_target_pairs={{0,4},{4,0},{8,12},{12,8},{16,20},{20,16},{24,28},{28,24},{1,5},{5... | collective-permute-start | bytes 55304 | tf_op jit(solution)/shard_map/ppermute | solution.py:54
  2.3 8.6 %collective-permute-start.3 = (bf16[6,6144]{1,0:T(8,128)(2,1)S(1)}, bf16[6,6144]{1,0:T(8,128)(2,1)S(1)}, u32[]{:S(2)}, u32[]{:S(2)}) collective-permute-start(bf16[6,6144]{1,0:T(8,128)(2,1)S(1)} %get-tuple-element.13.refs_3_), channel_id=1, source_target_pairs={{0,1},{1,0},{2,3},{3,2},{4,5},{5,4},{6,7},{7,6},{8,9},{9,8},{10,11... | collective-permute-start | bytes 221192 | tf_op jit(solution)/shard_map/ppermute | solution.py:54
  4.9 10.9 %collective-permute-start.1 = (bf16[6,6144]{1,0:T(8,128)(2,1)S(1)}, bf16[6,6144]{1,0:T(8,128)(2,1)S(1)}, u32[]{:S(2)}, u32[]{:S(2)}) collective-permute-start(bf16[6,6144]{1,0:T(8,128)(2,1)S(1)} %get-tuple-element.13.refs_3_), channel_id=1, source_target_pairs={{0,2},{1,3},{2,0},{3,1},{4,6},{5,7},{6,4},{7,5},{8,10},{9,11},{10,... | collective-permute-start | bytes 221192 | tf_op jit(solution)/shard_map/ppermute | solution.py:54
  7.5 8.3 %collective-permute-start = (bf16[6,6144]{1,0:T(8,128)(2,1)S(1)}, bf16[6,6144]{1,0:T(8,128)(2,1)S(1)}, u32[]{:S(2)}, u32[]{:S(2)}) collective-permute-start(bf16[6,6144]{1,0:T(8,128)(2,1)S(1)} %get-tuple-element.13.refs_3_), channel_id=1, source_target_pairs={{0,3},{1,2},{2,1},{3,0},{4,7},{5,6},{6,5},{7,4},{8,11},{9,10},{10,... | collective-permute-start | bytes 221192 | tf_op jit(solution)/shard_map/ppermute | solution.py:54
  7.6 8.3 %collective-permute-start.5 = (bf16[2,3,3072]{2,1,0:T(4,128)(2,1)S(1)}, bf16[2,3,3072]{2,1,0:T(4,128)(2,1)S(1)}, u32[]{:S(2)}, u32[]{:S(2)}) collective-permute-start(bf16[2,3,3072]{2,1,0:T(4,128)(2,1)S(1)} %pad_maximum_fusion.after.refs_4_), channel_id=1, source_target_pairs={{0,16},{4,20},{8,24},{12,28},{16,0},{20,4},{24,8},{28,12},{1,17},{... | collective-permute-start | bytes 110600 | tf_op jit(solution)/shard_map/ppermute | solution.py:54
  9.4 6.5 %collective-permute-start.4 = (bf16[2,3,3072]{2,1,0:T(4,128)(2,1)S(1)}, bf16[2,3,3072]{2,1,0:T(4,128)(2,1)S(1)}, u32[]{:S(2)}, u32[]{:S(2)}) collective-permute-start(bf16[2,3,3072]{2,1,0:T(4,128)(2,1)S(1)} %pad_maximum_fusion.after.refs_4_), channel_id=1, source_target_pairs={{0,8},{4,12},{8,0},{12,4},{16,24},{20,28},{24,16},{28,20},{1,9},{5... | collective-permute-start | bytes 110600 | tf_op jit(solution)/shard_map/ppermute | solution.py:54
  10.9 5.0 %collective-permute-start.6 = (bf16[2,3,3072]{2,1,0:T(4,128)(2,1)S(1)}, bf16[2,3,3072]{2,1,0:T(4,128)(2,1)S(1)}, u32[]{:S(2)}, u32[]{:S(2)}) collective-permute-start(bf16[2,3,3072]{2,1,0:T(4,128)(2,1)S(1)} %pad_maximum_fusion.after.refs_4_), channel_id=1, source_target_pairs={{0,24},{4,28},{8,16},{12,20},{16,8},{20,12},{24,0},{28,4},{1,25},{... | collective-permute-start | bytes 110600 | tf_op jit(solution)/shard_map/ppermute | solution.py:54
  32.3 2.2 %collective-permute-start.7 = (f32[4,3,3072]{2,1,0:T(4,128)S(1)}, f32[4,3,3072]{2,1,0:T(4,128)S(1)}, u32[]{:S(2)}, u32[]{:S(2)}) collective-permute-start(f32[4,3,3072]{2,1,0:T(4,128)S(1)} %get-tuple-element.22), channel_id=1, source_target_pairs={{0,4},{4,0},{8,12},{12,8},{16,20},{20,16},{24,28},{28,24},{1,5},{5... | collective-permute-start | bytes 442376 | tf_op jit(solution)/shard_map/ppermute | solution.py:54
  34.6 9.8 %collective-permute-start.8 = (f32[3,3072]{1,0:T(4,128)S(1)}, f32[3,3072]{1,0:T(4,128)S(1)}, u32[]{:S(2)}, u32[]{:S(2)}) collective-permute-start(f32[3,3072]{1,0:T(4,128)S(1)} %get-tuple-element.24), channel_id=1, source_target_pairs={{0,8},{4,12},{8,0},{12,4},{16,24},{20,28},{24,16},{28,20},{1,9},{5... | collective-permute-start | bytes 110600 | tf_op jit(solution)/shard_map/ppermute | solution.py:54
  36.4 8.0 %collective-permute-start.10 = (f32[3,3072]{1,0:T(4,128)S(1)}, f32[3,3072]{1,0:T(4,128)S(1)}, u32[]{:S(2)}, u32[]{:S(2)}) collective-permute-start(f32[3,3072]{1,0:T(4,128)S(1)} %get-tuple-element.25), channel_id=1, source_target_pairs={{0,24},{4,28},{8,16},{12,20},{16,8},{20,12},{24,0},{28,4},{1,25},{... | collective-permute-start | bytes 110600 | tf_op jit(solution)/shard_map/ppermute | solution.py:54
  37.9 6.5 %collective-permute-start.9 = (f32[3,3072]{1,0:T(4,128)S(1)}, f32[3,3072]{1,0:T(4,128)S(1)}, u32[]{:S(2)}, u32[]{:S(2)}) collective-permute-start(f32[3,3072]{1,0:T(4,128)S(1)} %get-tuple-element.26), channel_id=1, source_target_pairs={{0,16},{4,20},{8,24},{12,28},{16,0},{20,4},{24,8},{28,12},{1,17},{... | collective-permute-start | bytes 110600 | tf_op jit(solution)/shard_map/ppermute | solution.py:54

commit v5 on v4

--- a/solution.py
+++ b/solution.py
@@ -319,8 +319,7 @@
     hidden = [own] + [exchange(own, "batch", 4, k) for k in (1, 2, 3)]
     pair = jnp.stack([inputs, other])
     late, hidden[1] = lax.optimization_barrier((pair, hidden[1]))
-    pairs = [pair, exchange(pair, "mp", 8, 4), exchange(pair, "mp", 8, 2), exchange(late, "mp", 8, 6)]
-    pairs = [pairs[0], pairs[2], pairs[1], pairs[3]]
+    pairs = [pair, exchange(late, "mp", 8, 2), exchange(pair, "mp", 8, 4), exchange(pair, "mp", 8, 6)]
     early = load_part(0, 4, late, weight)
     grad, hidden, inputs, keep, send = both_part(hidden, pairs, weight, early)
 

time: 45.2 us -> 45.2 us (level)
  no operation moved by 1% of the time
where the time goes in v5:
time: 45.2 us; the launch traced here: 45 us
  Pallas kernels  30.5 us (67%)
  starting transfers between devices  12.9 us (29%)
  between operations  0.77 us (2%)
  other arithmetic  0.73 us (2%)
    pallas_call x1, Pallas kernels, both_part(): pl.pallas_call(both_kernel, in_specs=[VMEM] * 8 + [ANY, VMEM], out_specs=...  16.4 us
    ppermute x11, starting transfers between devices, exchange(): return lax.ppermute(x, axis, [(i, i ^ bits) for i in range(size)])  12.9 us
    pallas_call x2, Pallas kernels, weight_grad_part(): pl.pallas_call(functools.partial(weight_grad_kernel, first, count, block,...  8.28 us
    pallas_call x1, Pallas kernels, load_part(): pl.pallas_call(functools.partial(load_kernel, first), in_specs=[ANY, ANY]...  4.68 us
    pallas_call x1, Pallas kernels, hidden_part(): pl.pallas_call(hidden_kernel, in_specs=[ANY] * 3, out_specs=[VMEM] * 2, o...  1.12 us
  transfers between devices with their start and end apart: 11, of which 0 were waited for; matrix products, arithmetic and copies ran while one was open for 0% of the time, Pallas kernels for 29%

profile of v5, /device:TPU:0, one launch (start us, length us, event | category | flops | bytes accessed | tf_op | source)
XLA Modules:
  0.0 45.0 jit_solution(12056044437126865024)
XLA Ops:
  0.6 1.1 %hidden_part.1 = (bf16[6,6144]{1,0:T(8,128)(2,1)S(1)}, bf16[3,3072]{1,0:T(4,128)(2,1)S(1)}) custom-call(bf16[6,6144]{1,0:T(8,128)(2,1)} %pre_act.1, bf16[6,6144]{1,0:T(8,128)(2,1)} %out_grad.1, bf16[3,3072]{1,0:T(4,128)(2,1)} %inputs.1), custom_call_target="tpu_custom_call" | custom-call | tf_op jit(solution)/shard_map/hidden_part/pallas_call | solution.py:42
  1.8 0.5 %collective-permute-start.2 = (bf16[3,3072]{1,0:T(4,128)(2,1)S(1)}, bf16[3,3072]{1,0:T(4,128)(2,1)S(1)}, u32[]{:S(2)}, u32[]{:S(2)}) collective-permute-start(bf16[3,3072]{1,0:T(4,128)(2,1)S(1)} %get-tuple-element.14), channel_id=1, source_target_pairs={{0,4},{4,0},{8,12},{12,8},{16,20},{20,16},{24,28},{28,24},{1,5},{5... | collective-permute-start | bytes 55304 | tf_op jit(solution)/shard_map/ppermute | solution.py:54
  2.3 2.6 %collective-permute-start.3 = (bf16[6,6144]{1,0:T(8,128)(2,1)S(1)}, bf16[6,6144]{1,0:T(8,128)(2,1)S(1)}, u32[]{:S(2)}, u32[]{:S(2)}) collective-permute-start(bf16[6,6144]{1,0:T(8,128)(2,1)S(1)} %get-tuple-element.13.refs_3_), channel_id=1, source_target_pairs={{0,1},{1,0},{2,3},{3,2},{4,5},{5,4},{6,7},{7,6},{8,9},{9,8},{10,11... | collective-permute-start | bytes 221192 | tf_op jit(solution)/shard_map/ppermute | solution.py:54
  4.9 2.6 %collective-permute-start.1 = (bf16[6,6144]{1,0:T(8,128)(2,1)S(1)}, bf16[6,6144]{1,0:T(8,128)(2,1)S(1)}, u32[]{:S(2)}, u32[]{:S(2)}) collective-permute-start(bf16[6,6144]{1,0:T(8,128)(2,1)S(1)} %get-tuple-element.13.refs_3_), channel_id=1, source_target_pairs={{0,2},{1,3},{2,0},{3,1},{4,6},{5,7},{6,4},{7,5},{8,10},{9,11},{10,... | collective-permute-start | bytes 221192 | tf_op jit(solution)/shard_map/ppermute | solution.py:54
  7.5 0.0 collective-permute-start
  7.5 0.0 collective-permute-done.2
  7.6 2.7 %collective-permute-start.6 = (bf16[2,3,3072]{2,1,0:T(4,128)(2,1)S(1)}, bf16[2,3,3072]{2,1,0:T(4,128)(2,1)S(1)}, u32[]{:S(2)}, u32[]{:S(2)}) collective-permute-start(bf16[2,3,3072]{2,1,0:T(4,128)(2,1)S(1)} %pad_maximum_fusion.after.refs_4_), channel_id=1, source_target_pairs={{0,24},{4,28},{8,16},{12,20},{16,8},{20,12},{24,0},{28,4},{1,25},{... | collective-permute-start | bytes 110600 | tf_op jit(solution)/shard_map/ppermute | solution.py:54
  10.3 0.5 %collective-permute-start.5 = (bf16[2,3,3072]{2,1,0:T(4,128)(2,1)S(1)}, bf16[2,3,3072]{2,1,0:T(4,128)(2,1)S(1)}, u32[]{:S(2)}, u32[]{:S(2)}) collective-permute-start(bf16[2,3,3072]{2,1,0:T(4,128)(2,1)S(1)} %pad_maximum_fusion.after.refs_4_), channel_id=1, source_target_pairs={{0,16},{4,20},{8,24},{12,28},{16,0},{20,4},{24,8},{28,12},{1,17},{... | collective-permute-start | bytes 110600 | tf_op jit(solution)/shard_map/ppermute | solution.py:54
  10.8 0.0 collective-permute-done.3.refs_2_
  10.8 0.3 collective-permute-start.4
  11.1 4.7 %load_part.1.refs_9_ = bf16[4,256,6144]{2,1,0:T(8,128)(2,1)S(1)} custom-call(bf16[2,3,3072]{2,1,0:T(4,128)(2,1)S(1)} %pad_maximum_fusion.after.refs_4_, bf16[3072,6144]{1,0:T(8,128)(2,1)} %refs_8_.1), custom_call_target="tpu_custom_call" | custom-call | tf_op jit(solution)/shard_map/load_part/pallas_call | solution.py:81
  15.8 0.0 collective-permute-done.6.refs_7_
  15.8 0.0 collective-permute-done.5.refs_6_
  15.8 0.0 collective-permute-done.1.refs_1_
  15.8 0.0 collective-permute-done.refs_0_
  15.9 0.0 collective-permute-done.4.refs_5_
  15.9 16.4 %both_part.1 = (bf16[3072,6144]{1,0:T(8,128)(2,1)}, bf16[32,6144]{1,0:T(8,128)(2,1)S(1)}, bf16[32,3072]{1,0:T(8,128)(2,1)S(1)}, f32[4,3,3072]{2,1,0:T(4,128)S(1)}, f32[4,3,3072]{2,1,0:T(4,128)S(1)}) custom-call(bf16[6,6144]{1,0:T(8,128)(2,1)S(1)} %collective-permute-done.refs_0_, bf16[6,6144]{1,0:T(8,128)(2,1)S(1)} %collective-permute-done.1.refs_1_, ...), custom_call_target="tpu_custom_call" | custom-call | tf_op jit(solution)/shard_map/both_part/pallas_call | solution.py:232
  32.3 0.1 collective-permute-start.7
  32.4 2.1 %weight_grad_part.2.refs_0_ = bf16[3072,6144]{1,0:T(8,128)(2,1)} custom-call(bf16[32,3072]{1,0:T(8,128)(2,1)S(1)} %get-tuple-element.17.inputs, bf16[32,6144]{1,0:T(8,128)(2,1)S(1)} %get-tuple-element.18.hidden, bf16[3072,6144]{1,0:T(8,128)(2,1)} %get-tuple-element.19.refs_0_), custom_call_target="tpu_custom_call", output_to_operand_aliasing={{}: (2, {})} | custom-call | tf_op jit(solution)/shard_map/weight_grad_part/pallas_call | solution.py:299
  34.5 0.0 collective-permute-done.7
  34.5 0.1 add.12
  34.6 1.8 %collective-permute-start.8 = (f32[3,3072]{1,0:T(4,128)S(1)}, f32[3,3072]{1,0:T(4,128)S(1)}, u32[]{:S(2)}, u32[]{:S(2)}) collective-permute-start(f32[3,3072]{1,0:T(4,128)S(1)} %get-tuple-element.24), channel_id=1, source_target_pairs={{0,8},{4,12},{8,0},{12,4},{16,24},{20,28},{24,16},{28,20},{1,9},{5... | collective-permute-start | bytes 110600 | tf_op jit(solution)/shard_map/ppermute | solution.py:54
  36.4 1.5 %collective-permute-start.10 = (f32[3,3072]{1,0:T(4,128)S(1)}, f32[3,3072]{1,0:T(4,128)S(1)}, u32[]{:S(2)}, u32[]{:S(2)}) collective-permute-start(f32[3,3072]{1,0:T(4,128)S(1)} %get-tuple-element.25), channel_id=1, source_target_pairs={{0,24},{4,28},{8,16},{12,20},{16,8},{20,12},{24,0},{28,4},{1,25},{... | collective-permute-start | bytes 110600 | tf_op jit(solution)/shard_map/ppermute | solution.py:54
  37.9 0.3 collective-permute-start.9
  38.2 6.2 %weight_grad_part.3 = bf16[3072,6144]{1,0:T(8,128)(2,1)} custom-call(bf16[32,3072]{1,0:T(8,128)(2,1)S(1)} %get-tuple-element.17.inputs, bf16[32,6144]{1,0:T(8,128)(2,1)S(1)} %get-tuple-element.18.hidden, bf16[3072,6144]{1,0:T(8,128)(2,1)} %weight_grad_part.2.refs_0_), custom_call_target="tpu_custom_call", output_to_operand_aliasing={{}: (2, {})} | custom-call | tf_op jit(solution)/shard_map/weight_grad_part/pallas_call | solution.py:299
  44.4 0.0 collective-permute-done.8
  44.4 0.0 collective-permute-done.10
  44.4 0.0 collective-permute-done.9
  44.4 0.6 %fusion.3 = bf16[3,3072]{1,0:T(4,128)(2,1)} fusion(f32[3,3072]{1,0:T(4,128)S(1)} %collective-permute-done.10, f32[3,3072]{1,0:T(4,128)S(1)} %collective-permute-done.9, f32[3,3072]{1,0:T(4,128)S(1)} %collective-permute-done.8, f32[4,3,3072]{2,1,0:T(4,128)S(1)} %add.12), kind=kLoop, calls=%fused_computation.7 | loop fusion | flops 36864 | bytes 165888 | tf_op jit(solution)/shard_map/convert_element_type | solution.py:334
  (2 shorter events, 0.1 us)
Async XLA Ops:
  1.8 5.8 %collective-permute-start.2 = (bf16[3,3072]{1,0:T(4,128)(2,1)S(1)}, bf16[3,3072]{1,0:T(4,128)(2,1)S(1)}, u32[]{:S(2)}, u32[]{:S(2)}) collective-permute-start(bf16[3,3072]{1,0:T(4,128)(2,1)S(1)} %get-tuple-element.14), channel_id=1, source_target_pairs={{0,4},{4,0},{8,12},{12,8},{16,20},{20,16},{24,28},{28,24},{1,5},{5... | collective-permute-start | bytes 55304 | tf_op jit(solution)/shard_map/ppermute | solution.py:54
  2.3 8.5 %collective-permute-start.3 = (bf16[6,6144]{1,0:T(8,128)(2,1)S(1)}, bf16[6,6144]{1,0:T(8,128)(2,1)S(1)}, u32[]{:S(2)}, u32[]{:S(2)}) collective-permute-start(bf16[6,6144]{1,0:T(8,128)(2,1)S(1)} %get-tuple-element.13.refs_3_), channel_id=1, source_target_pairs={{0,1},{1,0},{2,3},{3,2},{4,5},{5,4},{6,7},{7,6},{8,9},{9,8},{10,11... | collective-permute-start | bytes 221192 | tf_op jit(solution)/shard_map/ppermute | solution.py:54
  4.9 10.9 %collective-permute-start.1 = (bf16[6,6144]{1,0:T(8,128)(2,1)S(1)}, bf16[6,6144]{1,0:T(8,128)(2,1)S(1)}, u32[]{:S(2)}, u32[]{:S(2)}) collective-permute-start(bf16[6,6144]{1,0:T(8,128)(2,1)S(1)} %get-tuple-element.13.refs_3_), channel_id=1, source_target_pairs={{0,2},{1,3},{2,0},{3,1},{4,6},{5,7},{6,4},{7,5},{8,10},{9,11},{10,... | collective-permute-start | bytes 221192 | tf_op jit(solution)/shard_map/ppermute | solution.py:54
  7.5 8.3 %collective-permute-start = (bf16[6,6144]{1,0:T(8,128)(2,1)S(1)}, bf16[6,6144]{1,0:T(8,128)(2,1)S(1)}, u32[]{:S(2)}, u32[]{:S(2)}) collective-permute-start(bf16[6,6144]{1,0:T(8,128)(2,1)S(1)} %get-tuple-element.13.refs_3_), channel_id=1, source_target_pairs={{0,3},{1,2},{2,1},{3,0},{4,7},{5,6},{6,5},{7,4},{8,11},{9,10},{10,... | collective-permute-start | bytes 221192 | tf_op jit(solution)/shard_map/ppermute | solution.py:54
  7.6 8.3 %collective-permute-start.6 = (bf16[2,3,3072]{2,1,0:T(4,128)(2,1)S(1)}, bf16[2,3,3072]{2,1,0:T(4,128)(2,1)S(1)}, u32[]{:S(2)}, u32[]{:S(2)}) collective-permute-start(bf16[2,3,3072]{2,1,0:T(4,128)(2,1)S(1)} %pad_maximum_fusion.after.refs_4_), channel_id=1, source_target_pairs={{0,24},{4,28},{8,16},{12,20},{16,8},{20,12},{24,0},{28,4},{1,25},{... | collective-permute-start | bytes 110600 | tf_op jit(solution)/shard_map/ppermute | solution.py:54
  10.3 5.5 %collective-permute-start.5 = (bf16[2,3,3072]{2,1,0:T(4,128)(2,1)S(1)}, bf16[2,3,3072]{2,1,0:T(4,128)(2,1)S(1)}, u32[]{:S(2)}, u32[]{:S(2)}) collective-permute-start(bf16[2,3,3072]{2,1,0:T(4,128)(2,1)S(1)} %pad_maximum_fusion.after.refs_4_), channel_id=1, source_target_pairs={{0,16},{4,20},{8,24},{12,28},{16,0},{20,4},{24,8},{28,12},{1,17},{... | collective-permute-start | bytes 110600 | tf_op jit(solution)/shard_map/ppermute | solution.py:54
  10.8 5.1 %collective-permute-start.4 = (bf16[2,3,3072]{2,1,0:T(4,128)(2,1)S(1)}, bf16[2,3,3072]{2,1,0:T(4,128)(2,1)S(1)}, u32[]{:S(2)}, u32[]{:S(2)}) collective-permute-start(bf16[2,3,3072]{2,1,0:T(4,128)(2,1)S(1)} %pad_maximum_fusion.after.refs_4_), channel_id=1, source_target_pairs={{0,8},{4,12},{8,0},{12,4},{16,24},{20,28},{24,16},{28,20},{1,9},{5... | collective-permute-start | bytes 110600 | tf_op jit(solution)/shard_map/ppermute | solution.py:54
  32.3 2.2 %collective-permute-start.7 = (f32[4,3,3072]{2,1,0:T(4,128)S(1)}, f32[4,3,3072]{2,1,0:T(4,128)S(1)}, u32[]{:S(2)}, u32[]{:S(2)}) collective-permute-start(f32[4,3,3072]{2,1,0:T(4,128)S(1)} %get-tuple-element.22), channel_id=1, source_target_pairs={{0,4},{4,0},{8,12},{12,8},{16,20},{20,16},{24,28},{28,24},{1,5},{5... | collective-permute-start | bytes 442376 | tf_op jit(solution)/shard_map/ppermute | solution.py:54
  34.6 9.8 %collective-permute-start.8 = (f32[3,3072]{1,0:T(4,128)S(1)}, f32[3,3072]{1,0:T(4,128)S(1)}, u32[]{:S(2)}, u32[]{:S(2)}) collective-permute-start(f32[3,3072]{1,0:T(4,128)S(1)} %get-tuple-element.24), channel_id=1, source_target_pairs={{0,8},{4,12},{8,0},{12,4},{16,24},{20,28},{24,16},{28,20},{1,9},{5... | collective-permute-start | bytes 110600 | tf_op jit(solution)/shard_map/ppermute | solution.py:54
  36.4 8.0 %collective-permute-start.10 = (f32[3,3072]{1,0:T(4,128)S(1)}, f32[3,3072]{1,0:T(4,128)S(1)}, u32[]{:S(2)}, u32[]{:S(2)}) collective-permute-start(f32[3,3072]{1,0:T(4,128)S(1)} %get-tuple-element.25), channel_id=1, source_target_pairs={{0,24},{4,28},{8,16},{12,20},{16,8},{20,12},{24,0},{28,4},{1,25},{... | collective-permute-start | bytes 110600 | tf_op jit(solution)/shard_map/ppermute | solution.py:54
  37.9 6.5 %collective-permute-start.9 = (f32[3,3072]{1,0:T(4,128)S(1)}, f32[3,3072]{1,0:T(4,128)S(1)}, u32[]{:S(2)}, u32[]{:S(2)}) collective-permute-start(f32[3,3072]{1,0:T(4,128)S(1)} %get-tuple-element.26), channel_id=1, source_target_pairs={{0,16},{4,20},{8,24},{12,28},{16,0},{20,4},{24,8},{28,12},{1,17},{... | collective-permute-start | bytes 110600 | tf_op jit(solution)/shard_map/ppermute | solution.py:54
